TPU v7x, 128 devices: a whole 4x4x4 slice. The times are simulated.
128 devices in a mesh: section: 4 (over x), head: 32 (over y, z, core).
Axes of the slice: x: 4, y: 4, z: 4, core: 2. Of those that a mesh axis runs over, the one named last changes fastest.
Arguments:
- token_ids: int32 [2, 12, 5], replicated, may hold values from 0 to 65535
- accepted: int32 [2, 12], replicated, may hold values from 1 to 5, 36 in all within a row
- embedding: bfloat16 [65536, 4096], P('section', 'head'), may hold values from -6 to 6
- norm_gain: float32 [4, 4096], P('section'), may hold values from 0.5 to 1.5
- w_gate: bfloat16 [4, 4096, 8192], P('section', None, 'head'), may hold values from -0.09375 to 0.09375
- w_input: bfloat16 [4, 4096, 8192], P('section', None, 'head'), may hold values from -0.09375 to 0.09375
- w_groups: bfloat16 [4, 4096, 2048], P('section', None, 'head'), may hold values from -0.046875 to 0.046875
- w_step: bfloat16 [4, 4096, 128], P('section', None, 'head'), may hold values from -0.09375 to 0.09375
- step_bias: float32 [4, 128], P('section', 'head'), may hold values from -4 to 1
- decay_rate: float32 [4, 128], P('section', 'head'), may hold values from 0.02 to 4
- skip_gain: float32 [4, 128], P('section', 'head'), may hold values from 0.5 to 1.5
- w_output: bfloat16 [4, 8192, 4096], P('section', 'head'), may hold values from -0.0625 to 0.0625
- states: bfloat16 [4, 12, 128, 64, 128], P('section', None, 'head'), may hold values from -4 to 4
- draft_gain: float32 [4096], replicated, may hold values from 0.5 to 1.5
- w_merge: bfloat16 [8192, 4096], P('section', 'head'), may hold values from -0.0625 to 0.0625
Outputs:
- kept_states: bfloat16 [4, 12, 128, 64, 128], P('section', None, 'head')
- draft_features: bfloat16 [72, 4096], P('section', 'head')
Inputs may be any that keep to these rules, and one draw needn't show every extreme that they name: accepted[r, b] is the count of one row b in one round r, between 1 and 5. For each round r, the 12 counts accepted[r, 0] .. accepted[r, 11] together sum to 36, and in each round at least one row keeps all 5 positions.
All inputs are finite; a program needn't handle non-finite values.
Results may differ from a plain program's by a relative error of at most 0.035.
Values may be sent and summed in bfloat16 or wider, within the bound.
No kernel may reach another device: no remote copies, remote signals or barrier semaphores. Data moves between devices by JAX's collectives and lax.ppermute only.
A program may use at most 128 MiB of HBM per device.

v0:
```python
import functools

import jax
import jax.numpy as jnp
from jax import lax
from jax.experimental import pallas as pl
from jax.experimental.pallas import tpu as pltpu
from jax.sharding import PartitionSpec as P

HEAD_DIM = 64
STATE = 128
GROUPS = 8
ACCEPTED = 36
POS = 5
ROWS = 12
PACKED = 2 * ACCEPTED
SLOTS = 80
WIDTH = 4096
CHUNK = 512
CELL = 128
SHARE = 24

epsilon = 1e-05
bf16 = jnp.bfloat16
f32 = jnp.float32

VMEM = pl.BlockSpec(memory_space=pltpu.VMEM)
SMEM = pl.BlockSpec(memory_space=pltpu.SMEM)
NT = (((1,), (1,)), ((), ()))
TN = (((0,), (0,)), ((), ()))


def route(value, target):
    pairs = []
    for source in range(128):
        goal = target(source >> 5, (source >> 3) & 3, (source >> 1) & 3, source & 1)
        if goal is not None:
            x, y, z, c = goal
            pairs.append((source, ((x & 3) << 5) | (y << 3) | (z << 1) | c))
    return lax.ppermute(value, ("section", "head"), pairs)


def over_core(value):
    return route(value, lambda x, y, z, c: (x, y, z, c ^ 1))


def over_z(value, e):
    return route(value, lambda x, y, z, c: (x, y, z ^ e, c))


def over_y(value, d):
    return route(value, lambda x, y, z, c: (x, y ^ d, z, c))


def over_x(value, s):
    return route(value, lambda x, y, z, c: (x ^ s, y, z, c))


def next_section(value, d):
    return route(value, lambda x, y, z, c: (x + 1, y ^ d, z, c))


def coordinates():
    head = lax.axis_index("head")
    return lax.axis_index("section"), head >> 3, (head >> 1) & 3, head & 1


def ends_of(accepted_ref):
    ends = []
    for r in range(2):
        total = 0
        row = []
        for b in range(ROWS):
            total = total + accepted_ref[r, b]
            row.append(total)
        ends.append(row)
    return ends


def owner_of(ends, slot):
    later = slot >= ACCEPTED
    inner = jnp.where(later, slot - ACCEPTED, slot)
    owner = jnp.zeros_like(slot)
    for b in range(ROWS):
        end = jnp.where(later, ends[1][b], ends[0][b])
        owner = owner + (inner >= end).astype(jnp.int32)
    return owner


def look_kernel(accepted_ref, tokens_ref, table_ref, out_ref, listed, held, sem):
    ends = ends_of(accepted_ref)
    vocab_local = table_ref.shape[0]
    base = lax.axis_index("section") * vocab_local
    for r in range(2):
        for b in range(ROWS):
            start = ends[r][b] - accepted_ref[r, b] + r * ACCEPTED
            for k in range(POS):
                listed[start + k] = tokens_ref[r, b, k]
    lane = lax.broadcasted_iota(jnp.int32, (1, CELL), 1)
    slot = lax.broadcasted_iota(jnp.int32, (SLOTS, CELL), 0)
    codes = []
    for g in range(PACKED // 8):
        code = jnp.full((1, CELL), -1, jnp.int32)
        for i in range(8):
            n = 8 * g + i
            local = listed[n] - base
            row = jnp.clip(local, 0, vocab_local - 1)
            block = pl.multiple_of((row >> 4) << 4, 16)
            pltpu.make_async_copy(
                table_ref.at[pl.ds(block, 16), :], held.at[pl.ds(16 * n, 16), :], sem
            ).start()
            code = jnp.where(lane == 16 * i + (row & 15), jnp.where(local == row, n, -1), code)
        codes.append(code)
    picks = [(slot == code).astype(bf16) for code in codes]
    pltpu.make_async_copy(table_ref.at[pl.ds(0, held.shape[0]), :], held, sem).wait()
    total = jnp.zeros((SLOTS, CELL), f32)
    for g, pick in enumerate(picks):
        total = total + jnp.dot(
            pick, held[g * CELL : (g + 1) * CELL, :], preferred_element_type=f32
        )
    out_ref[...] = total.astype(bf16)


def softplus(v):
    return jnp.maximum(v, 0.0) + jnp.log1p(jnp.exp(-jnp.abs(v)))


def fill_hidden(first, y, z, c, pieces, hidden):
    total = jnp.zeros((SLOTS, CELL), f32)
    for f in range(2):
        for e in range(4):
            if first:
                for d in range(4):
                    place = ((y ^ d) * 4 + (z ^ e)) * 2 + (c ^ f)
                    part = pieces[f][e, d]
                    hidden[:, pl.ds(pl.multiple_of(place * CELL, CELL), CELL)] = part
                    wide = part.astype(f32)
                    total = total + wide * wide
            else:
                place = (c ^ f) * 4 + (z ^ e)
                part = pieces[f][e]
                hidden[:, pl.ds(pl.multiple_of(place * CHUNK, CHUNK), CHUNK)] = part
                wide = part.astype(f32)
                square = wide * wide
                for i in range(CHUNK // CELL):
                    total = total + square[:, i * CELL : (i + 1) * CELL]
    return jnp.sum(total, axis=1, keepdims=True)


def share_rows(section):
    row = lax.broadcasted_iota(jnp.int32, (SHARE, SLOTS), 0)
    slot = lax.broadcasted_iota(jnp.int32, (SHARE, SLOTS), 1)
    return ((row < PACKED // 4) & (slot == section * (PACKED // 4) + row)).astype(bf16)


def project(last, gated, w_output, side, z, out_ref):
    for e in range(4):
        place = side * 4 + (e if last else z ^ e)
        w = w_output[:, pl.ds(pl.multiple_of(place * CHUNK, CHUNK), CHUNK)]
        part = jnp.dot(gated, w, preferred_element_type=f32).astype(out_ref.dtype)
        if last:
            for g in range(4):
                out_ref[g, :, e * CHUNK : (e + 1) * CHUNK] = part[g * SHARE : (g + 1) * SHARE]
        else:
            out_ref[e] = part


def keep_kernel(last, gated_ref, own_ref, w_output, out_ref):
    _, _, z, c = coordinates()
    project(last, gated_ref[...], w_output, c, z, out_ref)
    out_ref[0] += own_ref[...].astype(f32)


def layer_kernel(first, last, tick, *refs):
    (accepted_ref, bias_ref, rate_ref, skip_ref) = refs[:4]
    pieces = refs[4:6]
    (gain_ref, w_gate, w_input, w_pairs, w_step, w_output, states, place_ref) = refs[6:14]
    refs = refs[14:]
    if not first:
        old_x, old_b, old_decay = refs[:3]
        refs = refs[3:]
    gated_ref, own_ref, sent_ref, new_x, new_b, new_decay = refs[:6]
    hidden, normed = refs[-2:]
    x, y, z, c = coordinates()
    ends = ends_of(accepted_ref)

    squares = fill_hidden(first, y, z, c, pieces, hidden)
    scale = lax.rsqrt(squares * (1.0 / WIDTH) + epsilon)
    for i in range(WIDTH // CHUNK):
        at = slice(i * CHUNK, (i + 1) * CHUNK)
        normed[:, at] = (hidden[:, at].astype(f32) * scale * gain_ref[:, at]).astype(bf16)
    rows = normed[...]
    gate = jnp.dot(rows, w_gate[...], preferred_element_type=f32)
    inner = jnp.dot(rows, w_input[...], preferred_element_type=f32)
    pairs = lax.dot_general(rows, w_pairs[...], NT, preferred_element_type=f32).astype(bf16)
    pairs = jnp.dot(pairs, place_ref[...], preferred_element_type=f32).astype(bf16)
    b_vec, c_vec = pairs[:, :STATE], pairs[:, STATE:]
    raw = lax.dot_general(rows, w_step[...], NT, preferred_element_type=f32)

    lane = lax.broadcasted_iota(jnp.int32, (1, 16), 1)
    bias = jnp.zeros((1, 16), f32)
    rate = jnp.zeros((1, 16), f32)
    for h in range(4):
        bias = jnp.where(lane == h, bias_ref[0, h], bias)
        rate = jnp.where(lane == h, rate_ref[0, h], rate)
    step = softplus(raw + bias)
    fall = step * rate

    row_owner = owner_of(ends, lax.broadcasted_iota(jnp.int32, (SLOTS, SLOTS), 0))
    col_owner = owner_of(ends, lax.broadcasted_iota(jnp.int32, (SLOTS, SLOTS), 1))
    same = row_owner == col_owner
    ahead = lax.broadcasted_iota(jnp.int32, (SLOTS, SLOTS), 1) <= lax.broadcasted_iota(
        jnp.int32, (SLOTS, SLOTS), 0
    )
    causal = same & ahead
    causal_f32 = causal.astype(f32)
    log_decay = -jnp.dot(
        causal_f32, fall, precision=lax.Precision.HIGHEST, preferred_element_type=f32
    )
    log_decay_t = -lax.dot_general(
        fall,
        causal_f32,
        (((0,), (1,)), ((), ())),
        precision=lax.Precision.HIGHEST,
        preferred_element_type=f32,
    )
    after = (same & jnp.logical_not(ahead)).astype(f32)
    rest = -jnp.dot(after, fall, precision=lax.Precision.HIGHEST, preferred_element_type=f32)
    batch = lax.broadcasted_iota(jnp.int32, (16, SLOTS), 0)
    batch_owner = owner_of(ends, lax.broadcasted_iota(jnp.int32, (16, SLOTS), 1))
    total = -jnp.dot(
        (batch == batch_owner).astype(f32),
        fall,
        precision=lax.Precision.HIGHEST,
        preferred_element_type=f32,
    )

    products = lax.dot_general(c_vec, b_vec, NT, preferred_element_type=f32)
    slot_owner = owner_of(ends, lax.broadcasted_iota(jnp.int32, (SLOTS, STATE), 0))
    carried = jnp.zeros((SLOTS, 4 * HEAD_DIM), f32)
    for b in range(ROWS):
        mine = jnp.where(slot_owner == b, c_vec, jnp.zeros((), bf16))
        carried = carried + lax.dot_general(mine, states[b], NT, preferred_element_type=f32)

    wide_lane = lax.broadcasted_iota(jnp.int32, (SLOTS, 2 * HEAD_DIM), 1)
    left = wide_lane < HEAD_DIM

    def spread(v, p):
        return jnp.where(left, v[:, 2 * p : 2 * p + 1], v[:, 2 * p + 1 : 2 * p + 2])

    gated = []
    weighted = []
    for p in range(2):
        at = slice(p * 128, (p + 1) * 128)
        x_p = inner[:, at]
        dx = spread(step, p) * x_p
        dx_b = dx.astype(bf16)
        mixed = []
        for h in (2 * p, 2 * p + 1):
            gap = log_decay[:, h : h + 1] - log_decay_t[h : h + 1, :]
            weights = products * jnp.exp(jnp.where(causal, gap, -1e30))
            mixed.append(jnp.dot(weights.astype(bf16), dx_b, preferred_element_type=f32))
        out = jnp.where(left, mixed[0], mixed[1])
        out = out + jnp.exp(spread(log_decay, p)) * carried[:, at]
        skip = jnp.where(left, skip_ref[0, 2 * p], skip_ref[0, 2 * p + 1])
        out = out + skip * x_p
        g = gate[:, at]
        gated.append((out * (g / (1.0 + jnp.exp(-g)))).astype(bf16))
        weighted.append((jnp.exp(spread(rest, p)) * dx).astype(bf16))
    gated = jnp.concatenate(gated, axis=1)

    half = WIDTH // 2
    if last:
        order = jnp.concatenate([share_rows(z ^ e) for e in range(4)], axis=0)
        gated = jnp.dot(order, gated, preferred_element_type=f32).astype(bf16)
        own = hidden[:, pl.ds(pl.multiple_of(c * half, half), half)]
        own = jnp.dot(order[:SHARE], own, preferred_element_type=f32).astype(bf16)
    else:
        place = c * 4 + z
        own = hidden[:, pl.ds(pl.multiple_of(place * CHUNK, CHUNK), CHUNK)]
    gated_ref[...] = gated
    own_ref[...] = jnp.where(y == 0, own, jnp.zeros((), bf16))
    project(last, gated, w_output, c ^ 1, z, sent_ref)

    decay = jnp.exp(total)
    if first:
        share = share_rows(x)
        refs[6][...] = jnp.dot(share, hidden[...], preferred_element_type=f32).astype(bf16)
        new_x[:, :128] = weighted[0]
        new_x[:, 128:] = weighted[1]
        new_b[...] = b_vec
        new_decay[...] = decay
    else:
        now = x == tick
        new_x[:, :128] = jnp.where(now, weighted[0], old_x[:, :128])
        new_x[:, 128:] = jnp.where(now, weighted[1], old_x[:, 128:])
        new_b[...] = jnp.where(now, b_vec, old_b[...])
        new_decay[...] = jnp.where(now, decay, old_decay[...])


def state_kernel(accepted_ref, x_ref, b_ref, decay_ref, states, out_ref):
    ends = ends_of(accepted_ref)
    slot_owner = owner_of(ends, lax.broadcasted_iota(jnp.int32, (SLOTS, STATE), 0))
    x_all = x_ref[...]
    b_all = b_ref[...]
    for b in range(ROWS):
        mine = jnp.where(slot_owner == b, b_all, jnp.zeros((), bf16))
        added = lax.dot_general(x_all, mine, TN, preferred_element_type=f32)
        for h in range(4):
            at = slice(h * HEAD_DIM, (h + 1) * HEAD_DIM)
            scale = decay_ref[b : b + 1, h : h + 1]
            out_ref[b, at, :] = (states[b, at, :].astype(f32) * scale + added[at, :]).astype(bf16)


def add_products(x, rows, weights, low, total):
    half = WIDTH // 2
    w_own, w_far, w_pair = weights
    for way, w in ((0, w_own), (3, w_far), (1, w_pair.at[0]), (2, w_pair.at[1])):
        block = x ^ way

        @pl.when((block >= low) & (block < low + 2))
        def _():
            at = pl.ds(pl.multiple_of((block - low) * half, half), half)
            total[...] += jnp.dot(rows[:, at], w[...], preferred_element_type=f32)


def tokens_kernel(tokens_ref, *refs):
    out_ref = refs[3]
    out_ref[...] = jnp.zeros((SHARE, CELL), f32)
    add_products(lax.axis_index("section"), tokens_ref, refs[:3], 2, out_ref)


def merge_kernel(own_ref, other_ref, part_ref, gain_ref, *refs):
    out_ref, joined, total = refs[3:]
    x, _, _, c = coordinates()
    half = WIDTH // 2
    squares = jnp.zeros((SHARE, 1), f32)
    for ref in (own_ref, other_ref):
        wide = ref[...].astype(f32)
        squares = squares + jnp.sum(wide * wide, axis=1, keepdims=True)
    scale = lax.rsqrt(squares * (1.0 / WIDTH) + epsilon)
    for f, ref in enumerate((own_ref, other_ref)):
        at = pl.ds(pl.multiple_of((c ^ f) * half, half), half)
        joined[:, at] = (ref[...].astype(f32) * scale * gain_ref[:, at]).astype(bf16)
    total[...] = part_ref[...]
    add_products(x, joined, refs[:3], 0, total)
    out_ref[...] = total[: PACKED // 4, :].astype(bf16)


def turn_groups(w_groups, y, z):
    row = jnp.arange(64, dtype=jnp.int32)
    block, half, kind, entry = row // 16, (row // 8) % 2, (row // 4) % 2, row % 4
    group = (y ^ block) * 2 + ((z // 2) ^ half)
    column = (entry * 2 + kind) * 8 + group
    order = (column[:, None] == jnp.arange(64, dtype=jnp.int32)[None, :]).astype(bf16)
    return lax.dot_general(order, w_groups, NT, preferred_element_type=f32).astype(bf16)


def pair_places(y, z, c):
    row = jnp.arange(256, dtype=jnp.int32)
    f, e, d = row // 128, (row // 32) % 4, (row // 8) % 4
    kind, entry = (row // 4) % 2, row % 4
    source = ((y ^ d) * 4 + (z ^ e)) * 2 + (c ^ f)
    column = kind * STATE + source * 4 + entry
    return (column[:, None] == jnp.arange(256, dtype=jnp.int32)[None, :]).astype(bf16)


def shape(dims, kind):
    return jax.ShapeDtypeStruct(dims, kind)


PARAMS = pltpu.CompilerParams(vmem_limit_bytes=40 * 1024 * 1024)
KEEP_BYTES = 8 * 10**6
SMALL = pltpu.CompilerParams(vmem_limit_bytes=8 * 1024 * 1024)


def on_device(
    token_ids,
    accepted,
    embedding,
    norm_gain,
    w_gate,
    w_input,
    w_groups,
    w_step,
    step_bias,
    decay_rate,
    skip_gain,
    w_output,
    states,
    draft_gain,
    w_merge,
):
    x = lax.axis_index("section")
    head = lax.axis_index("head")
    y, z, c = head // 8, (head // 2) % 4, head % 2
    turned = turn_groups(w_groups[0], y, z)
    blocks = [turned[:16]] + [over_y(turned[16 * d : 16 * d + 16], d) for d in (1, 2, 3)]
    looked = pl.pallas_call(
        look_kernel,
        out_shape=shape((SLOTS, CELL), bf16),
        in_specs=[SMEM] * 2 + [pl.BlockSpec(memory_space=pl.ANY)],
        out_specs=VMEM,
        scratch_shapes=[
            pltpu.SMEM((2 * ROWS * POS,), jnp.int32),
            pltpu.VMEM((16 * PACKED, CELL), bf16),
            pltpu.SemaphoreType.DMA,
        ],
        cost_estimate=pl.CostEstimate(flops=10**9, bytes_accessed=10**7, transcendentals=0),
        compiler_params=SMALL,
        name="look",
    )(accepted, token_ids, embedding)
    looked, blocks, w_far = lax.optimization_barrier((looked, blocks, over_x(w_merge, 3)))
    found = [over_x(looked, s) for s in (1, 3, 2)]
    picked = looked.astype(f32)
    for part in found:
        picked = picked + part.astype(f32)
    picked = picked.astype(bf16)
    mine = jnp.concatenate([block[:8] for block in blocks], axis=0)
    other = jnp.concatenate([block[8:] for block in blocks], axis=0)
    pairs_half = [mine, over_z(mine, 1), over_z(other, 2), over_z(other, 3)]
    line = jnp.stack([picked] + [over_y(picked, d) for d in (1, 2, 3)])
    line, pairs_half = lax.optimization_barrier((line, pairs_half))
    pairs_half = jnp.concatenate(pairs_half, axis=0)
    w_pairs = jnp.concatenate([pairs_half, over_core(pairs_half)], axis=0)
    plane = jnp.stack([line] + [over_z(line, e) for e in (1, 2, 3)])

    pair_place = pair_places(y, z, c)
    step_rows = jnp.pad(w_step[0].T, ((0, 12), (0, 0)))
    start_states = states[0].reshape(ROWS, 4 * HEAD_DIM, STATE)
    pieces = (plane, over_core(plane))
    w_pair = jnp.stack([w_merge, w_far])

    saved_kinds = (
        shape((SLOTS, 4 * HEAD_DIM), bf16),
        shape((SLOTS, STATE), bf16),
        shape((16, 16), f32),
    )
    saved = ()
    for tick in range(4):
        first, last = tick == 0, tick == 3
        part = (4, SHARE, WIDTH // 2) if last else (4, SLOTS, CHUNK)
        kinds = (
            shape((4 * SHARE if last else SLOTS, 4 * HEAD_DIM), bf16),
            shape(part[1:], bf16),
            shape(part, bf16),
        ) + saved_kinds
        if first:
            kinds = kinds + (shape((SHARE, WIDTH), bf16),)
        gated, own, sent, *saved = pl.pallas_call(
            functools.partial(layer_kernel, first, last, tick),
            out_shape=kinds,
            in_specs=[SMEM] * 4 + [VMEM] * (10 + len(saved)),
            out_specs=(VMEM,) * len(kinds),
            scratch_shapes=[pltpu.VMEM((SLOTS, WIDTH), bf16)] * 2,
            compiler_params=PARAMS,
            name="layer",
        )(
            accepted,
            step_bias,
            decay_rate,
            skip_gain,
            *pieces,
            norm_gain,
            w_gate[0],
            w_input[0],
            w_pairs,
            step_rows,
            w_output[0],
            start_states,
            pair_place,
            *saved,
        )
        if first:
            tokens = saved.pop()
        kept = pl.pallas_call(
            functools.partial(keep_kernel, last),
            out_shape=shape(part, f32),
            in_specs=[VMEM] * 3,
            out_specs=VMEM,
            compiler_params=SMALL,
            cost_estimate=pl.CostEstimate(
                flops=10**8, bytes_accessed=KEEP_BYTES, transcendentals=0
            ),
            name="keep",
        )(gated, own, w_output[0])
        other = over_core(sent)
        if last:
            other, w_pair = lax.optimization_barrier((other, w_pair))
        summed = kept + other.astype(f32)
        across = [over_z(summed[e].astype(bf16), e) for e in (1, 2, 3)]
        total = summed[0]
        for part in across:
            total = total + part.astype(f32)
        total = total.astype(bf16)
        if last:
            break
        arrived = [next_section(total, d) for d in range(4)]
        own = arrived[0].astype(f32)
        for part in arrived[1:]:
            own = own + part.astype(f32)
        own = own.astype(bf16)
        if tick == 2:
            own, w_pair = lax.optimization_barrier((own, w_pair))
            w_pair = over_x(w_pair, 1)
        plane = jnp.stack([own] + [over_z(own, e) for e in (1, 2, 3)])
        pieces = (plane, over_core(plane))

    kept_states = pl.pallas_call(
        state_kernel,
        out_shape=shape((ROWS, 4 * HEAD_DIM, STATE), bf16),
        in_specs=[SMEM] + [VMEM] * 4,
        out_specs=VMEM,
        compiler_params=SMALL,
        name="kept",
    )(accepted, *saved, start_states)

    tokens_part = pl.pallas_call(
        tokens_kernel,
        out_shape=shape((SHARE, CELL), f32),
        in_specs=[VMEM] * 4,
        out_specs=VMEM,
        compiler_params=SMALL,
        name="tokens",
    )(tokens, w_merge, w_far, w_pair)
    parts = [over_y(total, d) for d in (1, 2, 3)]
    parts, kept_states, tokens_part = lax.optimization_barrier((parts, kept_states, tokens_part))
    final = total.astype(f32)
    for part in parts:
        final = final + part.astype(f32)
    final = final.astype(bf16)
    rows = [
        route(final, lambda x, y, z, c, k=k: (z, y, z ^ k, c) if x == 3 else None)
        for k in range(4)
    ]
    rows = (rows[0] + rows[1]) + (rows[2] + rows[3])
    draft = pl.pallas_call(
        merge_kernel,
        out_shape=shape((PACKED // 4, CELL), bf16),
        in_specs=[VMEM] * 7,
        out_specs=VMEM,
        scratch_shapes=[pltpu.VMEM((SHARE, WIDTH), bf16), pltpu.VMEM((SHARE, CELL), f32)],
        compiler_params=SMALL,
        name="merge",
    )(rows, over_core(rows), tokens_part, draft_gain.reshape(1, WIDTH), w_merge, w_far, w_pair)
    return (kept_states.reshape(1, ROWS, 4, HEAD_DIM, STATE), draft)


def solution(mesh):
    return jax.shard_map(
        on_device,
        mesh=mesh,
        in_specs=(
            P(),
            P(),
            P("section", "head"),
            P("section", None),
            P("section", None, "head"),
            P("section", None, "head"),
            P("section", None, "head"),
            P("section", None, "head"),
            P("section", "head"),
            P("section", "head"),
            P("section", "head"),
            P("section", "head", None),
            P("section", None, "head", None, None),
            P(),
            P("section", "head"),
        ),
        out_specs=(P("section", None, "head", None, None), P("section", "head")),
        check_vma=False,
    )
```

profile of v0, /device:TPU:33, one launch (start us, length us, event | category | flops | bytes accessed | tf_op | source)
XLA Modules:
  0.0 201.0 jit_solution(2825443006483572576)
XLA Ops:
  0.7 2.6 %collective-permute-start.3 = (bf16[2048,128]{1,0:T(8,128)(2,1)}, bf16[2048,128]{1,0:T(8,128)(2,1)S(1)}, u32[]{:S(2)}, u32[]{:S(2)}) collective-permute-start(bf16[2048,128]{1,0:T(8,128)(2,1)} %refs_0_.11), channel_id=1, source_target_pairs={{0,96},{1,97},{2,98},{3,99},{4,100},{5,101},{6,102},{7,103},{8,104... | collective-permute-start | bytes 1572872 | tf_op jit(solution)/shard_map/ppermute | solution.py:40
  5.0 2.6 %collective-permute-start.1 = (bf16[16,4096]{1,0:T(8,128)(2,1)S(1)}, bf16[16,4096]{1,0:T(8,128)(2,1)S(1)}, u32[]{:S(2)}, u32[]{:S(2)}) collective-permute-start(bf16[16,4096]{1,0:T(8,128)(2,1)S(1)} %get-tuple-element.101), channel_id=1, source_target_pairs={{0,16},{1,17},{2,18},{3,19},{4,20},{5,21},{6,22},{7,23},{8,24},{9,... | collective-permute-start | bytes 393224 | tf_op jit(solution)/shard_map/ppermute | solution.py:40
  12.7 2.8 %collective-permute-done.2 = bf16[16,4096]{1,0:T(8,128)(2,1)S(1)} collective-permute-done((bf16[16,4096]{1,0:T(8,128)(2,1)S(1)}, bf16[16,4096]{1,0:T(8,128)(2,1)S(1)}, u32[]{:S(2)}, u32[]{:S(2)}) %collective-permute-start.2) | collective-permute-done | bytes 131104 | tf_op jit(solution)/shard_map/ppermute | solution.py:40
  18.2 2.8 %collective-permute-start.11 = (bf16[32,4096]{1,0:T(8,128)(2,1)S(1)}, bf16[32,4096]{1,0:T(8,128)(2,1)S(1)}, u32[]{:S(2)}, u32[]{:S(2)}) collective-permute-start(bf16[32,4096]{1,0:T(8,128)(2,1)S(1)} %pad_maximum_fusion.7), channel_id=1, source_target_pairs={{0,4},{1,5},{2,6},{3,7},{4,0},{5,1},{6,2},{7,3},{8,12},{9,13},{10,... | collective-permute-start | bytes 786440 | tf_op jit(solution)/shard_map/ppermute | solution.py:40
  21.1 2.7 %collective-permute-start.9 = (bf16[80,128]{1,0:T(8,128)(2,1)S(1)}, bf16[80,128]{1,0:T(8,128)(2,1)S(1)}, u32[]{:S(2)}, u32[]{:S(2)}) collective-permute-start(bf16[80,128]{1,0:T(8,128)(2,1)S(1)} %add_convert_fusion.4), channel_id=1, source_target_pairs={{0,24},{1,25},{2,26},{3,27},{4,28},{5,29},{6,30},{7,31},{8,16},{9,... | collective-permute-start | bytes 61448 | tf_op jit(solution)/shard_map/ppermute | solution.py:40
  25.8 3.3 %collective-permute-done.8 = bf16[80,128]{1,0:T(8,128)(2,1)S(1)} collective-permute-done((bf16[80,128]{1,0:T(8,128)(2,1)S(1)}, bf16[80,128]{1,0:T(8,128)(2,1)S(1)}, u32[]{:S(2)}, u32[]{:S(2)}) %collective-permute-start.8) | collective-permute-done | bytes 20512 | tf_op jit(solution)/shard_map/ppermute | solution.py:40
  29.1 3.0 %collective-permute-done.10 = bf16[32,4096]{1,0:T(8,128)(2,1)S(1)} collective-permute-done((bf16[32,4096]{1,0:T(8,128)(2,1)S(1)}, bf16[32,4096]{1,0:T(8,128)(2,1)S(1)}, u32[]{:S(2)}, u32[]{:S(2)}) %collective-permute-start.10) | collective-permute-done | bytes 262176 | tf_op jit(solution)/shard_map/ppermute | solution.py:40
  43.8 4.6 %layer.4 = (bf16[80,256]{1,0:T(8,128)(2,1)S(1)}, bf16[80,512]{1,0:T(8,128)(2,1)S(1)}, bf16[4,80,512]{2,1,0:T(8,128)(2,1)S(1)}, bf16[80,256]{1,0:T(8,128)(2,1)S(1...) custom-call(s32[2,12]{1,0:T(2,128)S(1)} %copy-done.8, f32[1,4]{1,0:T(1,128)S(1)} %copy-done.10, ...), custom_call_target="tpu_custom_call" | custom-call | tf_op jit(solution)/shard_map/layer/pallas_call | solution.py:450
  51.9 2.3 %collective-permute-start.20 = (bf16[80,512]{1,0:T(8,128)(2,1)S(1)}, bf16[80,512]{1,0:T(8,128)(2,1)S(1)}, u32[]{:S(2)}, u32[]{:S(2)}) collective-permute-start(bf16[80,512]{1,0:T(8,128)(2,1)S(1)} %get-tuple-element.115), channel_id=1, source_target_pairs={{0,4},{1,5},{2,6},{3,7},{4,0},{5,1},{6,2},{7,3},{8,12},{9,13},{10,... | collective-permute-start | bytes 245768 | tf_op jit(solution)/shard_map/ppermute | solution.py:40
  54.2 2.5 %collective-permute-done.20 = bf16[80,512]{1,0:T(8,128)(2,1)S(1)} collective-permute-done((bf16[80,512]{1,0:T(8,128)(2,1)S(1)}, bf16[80,512]{1,0:T(8,128)(2,1)S(1)}, u32[]{:S(2)}, u32[]{:S(2)}) %collective-permute-start.20) | collective-permute-done | bytes 81952 | tf_op jit(solution)/shard_map/ppermute | solution.py:40
  57.9 3.3 %collective-permute-start.25 = (bf16[80,512]{1,0:T(8,128)(2,1)S(1)}, bf16[80,512]{1,0:T(8,128)(2,1)S(1)}, u32[]{:S(2)}, u32[]{:S(2)}) collective-permute-start(bf16[80,512]{1,0:T(8,128)(2,1)S(1)} %fusion.17), channel_id=1, source_target_pairs={{0,56},{1,57},{2,58},{3,59},{4,60},{5,61},{6,62},{7,63},{8,48},{9,... | collective-permute-start | bytes 245768 | tf_op jit(solution)/shard_map/ppermute | solution.py:40
  64.6 3.5 %collective-permute-done.24 = bf16[80,512]{1,0:T(8,128)(2,1)S(1)} collective-permute-done((bf16[80,512]{1,0:T(8,128)(2,1)S(1)}, bf16[80,512]{1,0:T(8,128)(2,1)S(1)}, u32[]{:S(2)}, u32[]{:S(2)}) %collective-permute-start.24) | collective-permute-done | bytes 81952 | tf_op jit(solution)/shard_map/ppermute | solution.py:40
  73.6 2.6 %collective-permute-done.27 = bf16[80,512]{1,0:T(8,128)(2,1)S(1)} collective-permute-done((bf16[80,512]{1,0:T(8,128)(2,1)S(1)}, bf16[80,512]{1,0:T(8,128)(2,1)S(1)}, u32[]{:S(2)}, u32[]{:S(2)}) %collective-permute-start.27) | collective-permute-done | bytes 81952 | tf_op jit(solution)/shard_map/ppermute | solution.py:40
  77.1 3.3 %collective-permute-start.29 = (bf16[4,80,512]{2,1,0:T(8,128)(2,1)S(1)}, bf16[4,80,512]{2,1,0:T(8,128)(2,1)S(1)}, u32[]{:S(2)}, u32[]{:S(2)}) collective-permute-start(bf16[4,80,512]{2,1,0:T(8,128)(2,1)S(1)} %pad_maximum_fusion.3.refs_4_), channel_id=1, source_target_pairs={{0,1},{1,0},{2,3},{3,2},{4,5},{5,4},{6,7},{7,6},{8,9},{9,8},{10,11... | collective-permute-start | bytes 983048 | tf_op jit(solution)/shard_map/ppermute | solution.py:40
  81.6 4.4 %layer.5 = (bf16[80,256]{1,0:T(8,128)(2,1)S(1)}, bf16[80,512]{1,0:T(8,128)(2,1)S(1)}, bf16[4,80,512]{2,1,0:T(8,128)(2,1)S(1)}, bf16[80,256]{1,0:T(8,128)(2,1)S(1...) custom-call(s32[2,12]{1,0:T(2,128)S(1)} %copy-done.8, f32[1,4]{1,0:T(1,128)S(1)} %copy-done.10, ...), custom_call_target="tpu_custom_call" | custom-call | tf_op jit(solution)/shard_map/layer/pallas_call | solution.py:450
  101.8 2.5 %collective-permute-done.36 = bf16[80,512]{1,0:T(8,128)(2,1)S(1)} collective-permute-done((bf16[80,512]{1,0:T(8,128)(2,1)S(1)}, bf16[80,512]{1,0:T(8,128)(2,1)S(1)}, u32[]{:S(2)}, u32[]{:S(2)}) %collective-permute-start.36) | collective-permute-done | bytes 81952 | tf_op jit(solution)/shard_map/ppermute | solution.py:40
  112.3 3.8 %collective-permute-start.41 = (bf16[4,80,512]{2,1,0:T(8,128)(2,1)S(1)}, bf16[4,80,512]{2,1,0:T(8,128)(2,1)S(1)}, u32[]{:S(2)}, u32[]{:S(2)}) collective-permute-start(bf16[4,80,512]{2,1,0:T(8,128)(2,1)S(1)} %pad_maximum_fusion.4.refs_4_), channel_id=1, source_target_pairs={{0,1},{1,0},{2,3},{3,2},{4,5},{5,4},{6,7},{7,6},{8,9},{9,8},{10,11... | collective-permute-start | bytes 983048 | tf_op jit(solution)/shard_map/ppermute | solution.py:40
  117.3 4.4 %layer.6 = (bf16[80,256]{1,0:T(8,128)(2,1)S(1)}, bf16[80,512]{1,0:T(8,128)(2,1)S(1)}, bf16[4,80,512]{2,1,0:T(8,128)(2,1)S(1)}, bf16[80,256]{1,0:T(8,128)(2,1)S(1...) custom-call(s32[2,12]{1,0:T(2,128)S(1)} %copy-done.8, f32[1,4]{1,0:T(1,128)S(1)} %copy-done.10, ...), custom_call_target="tpu_custom_call" | custom-call | tf_op jit(solution)/shard_map/layer/pallas_call | solution.py:450
  137.5 2.6 %collective-permute-done.48 = bf16[80,512]{1,0:T(8,128)(2,1)S(1)} collective-permute-done((bf16[80,512]{1,0:T(8,128)(2,1)S(1)}, bf16[80,512]{1,0:T(8,128)(2,1)S(1)}, u32[]{:S(2)}, u32[]{:S(2)}) %collective-permute-start.48) | collective-permute-done | bytes 81952 | tf_op jit(solution)/shard_map/ppermute | solution.py:40
  147.7 4.2 %collective-permute-start.53 = (bf16[4,80,512]{2,1,0:T(8,128)(2,1)S(1)}, bf16[4,80,512]{2,1,0:T(8,128)(2,1)S(1)}, u32[]{:S(2)}, u32[]{:S(2)}) collective-permute-start(bf16[4,80,512]{2,1,0:T(8,128)(2,1)S(1)} %pad_maximum_fusion.5.refs_4_), channel_id=1, source_target_pairs={{0,1},{1,0},{2,3},{3,2},{4,5},{5,4},{6,7},{7,6},{8,9},{9,8},{10,11... | collective-permute-start | bytes 983048 | tf_op jit(solution)/shard_map/ppermute | solution.py:40
  153.2 4.6 %layer.7 = (bf16[96,256]{1,0:T(8,128)(2,1)S(1)}, bf16[24,2048]{1,0:T(8,128)(2,1)S(1)}, bf16[4,24,2048]{2,1,0:T(8,128)(2,1)S(1)}, bf16[80,256]{1,0:T(8,128)(2,1)S...) custom-call(s32[2,12]{1,0:T(2,128)S(1)} %copy-done.8, f32[1,4]{1,0:T(1,128)S(1)} %copy-done.10, ...), custom_call_target="tpu_custom_call" | custom-call | tf_op jit(solution)/shard_map/layer/pallas_call | solution.py:450
  159.6 4.4 %collective-permute-done.55.refs_2_ = bf16[2,2048,128]{2,1,0:T(8,128)(2,1)S(1)} collective-permute-done((bf16[2,2048,128]{2,1,0:T(8,128)(2,1)S(1)}, bf16[2,2048,128]{2,1,0:T(8,128)(2,1)S(1)}, u32[]{:S(2)}, u32[]{:S(2)}) %collective-permute-start.55) | collective-permute-done | bytes 1048608 | tf_op jit(solution)/shard_map/ppermute | solution.py:40
  182.3 9.7 %collective-permute-done.63 = bf16[24,2048]{1,0:T(8,128)(2,1)S(1)} collective-permute-done((bf16[24,2048]{1,0:T(8,128)(2,1)S(1)}, bf16[24,2048]{1,0:T(8,128)(2,1)S(1)}, u32[]{:S(2)}, u32[]{:S(2)}) %collective-permute-start.63) | collective-permute-done | bytes 98336 | tf_op jit(solution)/shard_map/ppermute | solution.py:40
  192.1 6.8 %collective-permute-start.66 = (bf16[24,2048]{1,0:T(8,128)(2,1)S(1)}, bf16[24,2048]{1,0:T(8,128)(2,1)S(1)}, u32[]{:S(2)}, u32[]{:S(2)}) collective-permute-start(bf16[24,2048]{1,0:T(8,128)(2,1)S(1)} %add_add_fusion.own_ref), channel_id=1, source_target_pairs={{0,1},{1,0},{2,3},{3,2},{4,5},{5,4},{6,7},{7,6},{8,9},{9,8},{10,11... | collective-permute-start | bytes 294920 | tf_op jit(solution)/shard_map/ppermute | solution.py:40
  (193 shorter events, 110.5 us)
Async XLA Ops:
  0.7 14.8 %collective-permute-start.3 = (bf16[2048,128]{1,0:T(8,128)(2,1)}, bf16[2048,128]{1,0:T(8,128)(2,1)S(1)}, u32[]{:S(2)}, u32[]{:S(2)}) collective-permute-start(bf16[2048,128]{1,0:T(8,128)(2,1)} %refs_0_.11), channel_id=1, source_target_pairs={{0,96},{1,97},{2,98},{3,99},{4,100},{5,101},{6,102},{7,103},{8,104... | collective-permute-start | bytes 1572872 | tf_op jit(solution)/shard_map/ppermute | solution.py:40
  3.6 8.6 %collective-permute-start = (bf16[16,4096]{1,0:T(8,128)(2,1)S(1)}, bf16[16,4096]{1,0:T(8,128)(2,1)S(1)}, u32[]{:S(2)}, u32[]{:S(2)}) collective-permute-start(bf16[16,4096]{1,0:T(8,128)(2,1)S(1)} %get-tuple-element.102), channel_id=1, source_target_pairs={{0,8},{1,9},{2,10},{3,11},{4,12},{5,13},{6,14},{7,15},{8,0},{9,1},... | collective-permute-start | bytes 393224 | tf_op jit(solution)/shard_map/ppermute | solution.py:40
  5.0 7.7 %collective-permute-start.1 = (bf16[16,4096]{1,0:T(8,128)(2,1)S(1)}, bf16[16,4096]{1,0:T(8,128)(2,1)S(1)}, u32[]{:S(2)}, u32[]{:S(2)}) collective-permute-start(bf16[16,4096]{1,0:T(8,128)(2,1)S(1)} %get-tuple-element.101), channel_id=1, source_target_pairs={{0,16},{1,17},{2,18},{3,19},{4,20},{5,21},{6,22},{7,23},{8,24},{9,... | collective-permute-start | bytes 393224 | tf_op jit(solution)/shard_map/ppermute | solution.py:40
  7.6 7.9 %collective-permute-start.2 = (bf16[16,4096]{1,0:T(8,128)(2,1)S(1)}, bf16[16,4096]{1,0:T(8,128)(2,1)S(1)}, u32[]{:S(2)}, u32[]{:S(2)}) collective-permute-start(bf16[16,4096]{1,0:T(8,128)(2,1)S(1)} %get-tuple-element.100), channel_id=1, source_target_pairs={{0,24},{1,25},{2,26},{3,27},{4,28},{5,29},{6,30},{7,31},{8,16},{9,... | collective-permute-start | bytes 393224 | tf_op jit(solution)/shard_map/ppermute | solution.py:40
  15.5 5.5 %collective-permute-start.6 = (bf16[80,128]{1,0:T(8,128)(2,1)S(1)}, bf16[80,128]{1,0:T(8,128)(2,1)S(1)}, u32[]{:S(2)}, u32[]{:S(2)}) collective-permute-start(bf16[80,128]{1,0:T(8,128)(2,1)S(1)} %look.1), channel_id=1, source_target_pairs={{0,64},{1,65},{2,66},{3,67},{4,68},{5,69},{6,70},{7,71},{8,72},{9,... | collective-permute-start | bytes 61448 | tf_op jit(solution)/shard_map/ppermute | solution.py:40
  18.2 13.9 %collective-permute-start.11 = (bf16[32,4096]{1,0:T(8,128)(2,1)S(1)}, bf16[32,4096]{1,0:T(8,128)(2,1)S(1)}, u32[]{:S(2)}, u32[]{:S(2)}) collective-permute-start(bf16[32,4096]{1,0:T(8,128)(2,1)S(1)} %pad_maximum_fusion.7), channel_id=1, source_target_pairs={{0,4},{1,5},{2,6},{3,7},{4,0},{5,1},{6,2},{7,3},{8,12},{9,13},{10,... | collective-permute-start | bytes 786440 | tf_op jit(solution)/shard_map/ppermute | solution.py:40
  21.0 12.6 %collective-permute-start.12 = (bf16[32,4096]{1,0:T(8,128)(2,1)S(1)}, bf16[32,4096]{1,0:T(8,128)(2,1)S(1)}, u32[]{:S(2)}, u32[]{:S(2)}) collective-permute-start(bf16[32,4096]{1,0:T(8,128)(2,1)S(1)} %pad_maximum_fusion.7), channel_id=1, source_target_pairs={{0,6},{1,7},{2,4},{3,5},{4,2},{5,3},{6,0},{7,1},{8,14},{9,15},{10,... | collective-permute-start | bytes 786440 | tf_op jit(solution)/shard_map/ppermute | solution.py:40
  23.8 8.4 %collective-permute-start.10 = (bf16[32,4096]{1,0:T(8,128)(2,1)S(1)}, bf16[32,4096]{1,0:T(8,128)(2,1)S(1)}, u32[]{:S(2)}, u32[]{:S(2)}) collective-permute-start(bf16[32,4096]{1,0:T(8,128)(2,1)S(1)} %pad_maximum_fusion.6), channel_id=1, source_target_pairs={{0,2},{1,3},{2,0},{3,1},{4,6},{5,7},{6,4},{7,5},{8,10},{9,11},{10,... | collective-permute-start | bytes 786440 | tf_op jit(solution)/shard_map/ppermute | solution.py:40
  57.9 6.7 %collective-permute-start.25 = (bf16[80,512]{1,0:T(8,128)(2,1)S(1)}, bf16[80,512]{1,0:T(8,128)(2,1)S(1)}, u32[]{:S(2)}, u32[]{:S(2)}) collective-permute-start(bf16[80,512]{1,0:T(8,128)(2,1)S(1)} %fusion.17), channel_id=1, source_target_pairs={{0,56},{1,57},{2,58},{3,59},{4,60},{5,61},{6,62},{7,63},{8,48},{9,... | collective-permute-start | bytes 245768 | tf_op jit(solution)/shard_map/ppermute | solution.py:40
  61.1 6.9 %collective-permute-start.24 = (bf16[80,512]{1,0:T(8,128)(2,1)S(1)}, bf16[80,512]{1,0:T(8,128)(2,1)S(1)}, u32[]{:S(2)}, u32[]{:S(2)}) collective-permute-start(bf16[80,512]{1,0:T(8,128)(2,1)S(1)} %fusion.17), channel_id=1, source_target_pairs={{0,48},{1,49},{2,50},{3,51},{4,52},{5,53},{6,54},{7,55},{8,56},{9,... | collective-permute-start | bytes 245768 | tf_op jit(solution)/shard_map/ppermute | solution.py:40
  62.2 5.8 %collective-permute-start.23 = (bf16[80,512]{1,0:T(8,128)(2,1)S(1)}, bf16[80,512]{1,0:T(8,128)(2,1)S(1)}, u32[]{:S(2)}, u32[]{:S(2)}) collective-permute-start(bf16[80,512]{1,0:T(8,128)(2,1)S(1)} %fusion.17), channel_id=1, source_target_pairs={{0,40},{1,41},{2,42},{3,43},{4,44},{5,45},{6,46},{7,47},{8,32},{9,... | collective-permute-start | bytes 245768 | tf_op jit(solution)/shard_map/ppermute | solution.py:40
  63.3 6.9 %collective-permute-start.22 = (bf16[80,512]{1,0:T(8,128)(2,1)S(1)}, bf16[80,512]{1,0:T(8,128)(2,1)S(1)}, u32[]{:S(2)}, u32[]{:S(2)}) collective-permute-start(bf16[80,512]{1,0:T(8,128)(2,1)S(1)} %fusion.17), channel_id=1, source_target_pairs={{0,32},{1,33},{2,34},{3,35},{4,36},{5,37},{6,38},{7,39},{8,40},{9,... | collective-permute-start | bytes 245768 | tf_op jit(solution)/shard_map/ppermute | solution.py:40
  95.1 6.7 %collective-permute-start.37 = (bf16[80,512]{1,0:T(8,128)(2,1)S(1)}, bf16[80,512]{1,0:T(8,128)(2,1)S(1)}, u32[]{:S(2)}, u32[]{:S(2)}) collective-permute-start(bf16[80,512]{1,0:T(8,128)(2,1)S(1)} %fusion.13), channel_id=1, source_target_pairs={{0,56},{1,57},{2,58},{3,59},{4,60},{5,61},{6,62},{7,63},{8,48},{9,... | collective-permute-start | bytes 245768 | tf_op jit(solution)/shard_map/ppermute | solution.py:40
  96.4 7.9 %collective-permute-start.36 = (bf16[80,512]{1,0:T(8,128)(2,1)S(1)}, bf16[80,512]{1,0:T(8,128)(2,1)S(1)}, u32[]{:S(2)}, u32[]{:S(2)}) collective-permute-start(bf16[80,512]{1,0:T(8,128)(2,1)S(1)} %fusion.13), channel_id=1, source_target_pairs={{0,48},{1,49},{2,50},{3,51},{4,52},{5,53},{6,54},{7,55},{8,56},{9,... | collective-permute-start | bytes 245768 | tf_op jit(solution)/shard_map/ppermute | solution.py:40
  97.3 7.0 %collective-permute-start.35 = (bf16[80,512]{1,0:T(8,128)(2,1)S(1)}, bf16[80,512]{1,0:T(8,128)(2,1)S(1)}, u32[]{:S(2)}, u32[]{:S(2)}) collective-permute-start(bf16[80,512]{1,0:T(8,128)(2,1)S(1)} %fusion.13), channel_id=1, source_target_pairs={{0,40},{1,41},{2,42},{3,43},{4,44},{5,45},{6,46},{7,47},{8,32},{9,... | collective-permute-start | bytes 245768 | tf_op jit(solution)/shard_map/ppermute | solution.py:40
  99.0 6.8 %collective-permute-start.34 = (bf16[80,512]{1,0:T(8,128)(2,1)S(1)}, bf16[80,512]{1,0:T(8,128)(2,1)S(1)}, u32[]{:S(2)}, u32[]{:S(2)}) collective-permute-start(bf16[80,512]{1,0:T(8,128)(2,1)S(1)} %fusion.13), channel_id=1, source_target_pairs={{0,32},{1,33},{2,34},{3,35},{4,36},{5,37},{6,38},{7,39},{8,40},{9,... | collective-permute-start | bytes 245768 | tf_op jit(solution)/shard_map/ppermute | solution.py:40
  130.6 6.9 %collective-permute-start.49 = (bf16[80,512]{1,0:T(8,128)(2,1)S(1)}, bf16[80,512]{1,0:T(8,128)(2,1)S(1)}, u32[]{:S(2)}, u32[]{:S(2)}) collective-permute-start(bf16[80,512]{1,0:T(8,128)(2,1)S(1)} %fusion.9), channel_id=1, source_target_pairs={{0,56},{1,57},{2,58},{3,59},{4,60},{5,61},{6,62},{7,63},{8,48},{9,... | collective-permute-start | bytes 245768 | tf_op jit(solution)/shard_map/ppermute | solution.py:40
  132.5 7.7 %collective-permute-start.48 = (bf16[80,512]{1,0:T(8,128)(2,1)S(1)}, bf16[80,512]{1,0:T(8,128)(2,1)S(1)}, u32[]{:S(2)}, u32[]{:S(2)}) collective-permute-start(bf16[80,512]{1,0:T(8,128)(2,1)S(1)} %fusion.9), channel_id=1, source_target_pairs={{0,48},{1,49},{2,50},{3,51},{4,52},{5,53},{6,54},{7,55},{8,56},{9,... | collective-permute-start | bytes 245768 | tf_op jit(solution)/shard_map/ppermute | solution.py:40
  133.1 7.1 %collective-permute-start.47 = (bf16[80,512]{1,0:T(8,128)(2,1)S(1)}, bf16[80,512]{1,0:T(8,128)(2,1)S(1)}, u32[]{:S(2)}, u32[]{:S(2)}) collective-permute-start(bf16[80,512]{1,0:T(8,128)(2,1)S(1)} %fusion.9), channel_id=1, source_target_pairs={{0,40},{1,41},{2,42},{3,43},{4,44},{5,45},{6,46},{7,47},{8,32},{9,... | collective-permute-start | bytes 245768 | tf_op jit(solution)/shard_map/ppermute | solution.py:40
  134.6 6.6 %collective-permute-start.46 = (bf16[80,512]{1,0:T(8,128)(2,1)S(1)}, bf16[80,512]{1,0:T(8,128)(2,1)S(1)}, u32[]{:S(2)}, u32[]{:S(2)}) collective-permute-start(bf16[80,512]{1,0:T(8,128)(2,1)S(1)} %fusion.9), channel_id=1, source_target_pairs={{0,32},{1,33},{2,34},{3,35},{4,36},{5,37},{6,38},{7,39},{8,40},{9,... | collective-permute-start | bytes 245768 | tf_op jit(solution)/shard_map/ppermute | solution.py:40
  141.2 22.8 %collective-permute-start.55 = (bf16[2,2048,128]{2,1,0:T(8,128)(2,1)S(1)}, bf16[2,2048,128]{2,1,0:T(8,128)(2,1)S(1)}, u32[]{:S(2)}, u32[]{:S(2)}) collective-permute-start(bf16[2,2048,128]{2,1,0:T(8,128)(2,1)S(1)} %pad_maximum_fusion.1), channel_id=1, source_target_pairs={{0,32},{1,33},{2,34},{3,35},{4,36},{5,37},{6,38},{7,39},{8,40},{9,... | collective-permute-start | bytes 3145736 | tf_op jit(solution)/shard_map/ppermute | solution.py:40
  170.9 6.2 %collective-permute-start.59 = (bf16[24,2048]{1,0:T(8,128)(2,1)S(1)}, bf16[24,2048]{1,0:T(8,128)(2,1)S(1)}, u32[]{:S(2)}, u32[]{:S(2)}) collective-permute-start(bf16[24,2048]{1,0:T(8,128)(2,1)S(1)} %fusion.5), channel_id=1, source_target_pairs={{0,8},{1,9},{2,10},{3,11},{4,12},{5,13},{6,14},{7,15},{8,0},{9,1},... | collective-permute-start | bytes 294920 | tf_op jit(solution)/shard_map/ppermute | solution.py:40
  181.0 11.1 %collective-permute-start.63 = (bf16[24,2048]{1,0:T(8,128)(2,1)S(1)}, bf16[24,2048]{1,0:T(8,128)(2,1)S(1)}, u32[]{:S(2)}, u32[]{:S(2)}) collective-permute-start(bf16[24,2048]{1,0:T(8,128)(2,1)S(1)} %add_convert_fusion), channel_id=1, source_target_pairs={{96,2},{97,3},{98,32},{99,33},{100,70},{101,71},{102,100},{103,101... | collective-permute-start | bytes 294920 | tf_op jit(solution)/shard_map/ppermute | solution.py:40
  192.1 7.7 %collective-permute-start.66 = (bf16[24,2048]{1,0:T(8,128)(2,1)S(1)}, bf16[24,2048]{1,0:T(8,128)(2,1)S(1)}, u32[]{:S(2)}, u32[]{:S(2)}) collective-permute-start(bf16[24,2048]{1,0:T(8,128)(2,1)S(1)} %add_add_fusion.own_ref), channel_id=1, source_target_pairs={{0,1},{1,0},{2,3},{3,2},{4,5},{5,4},{6,7},{7,6},{8,9},{9,8},{10,11... | collective-permute-start | bytes 294920 | tf_op jit(solution)/shard_map/ppermute | solution.py:40
  (58 other events, 299.7 us)
where the time goes:
time: 201 us
  starting transfers between devices  93.1 us (46%)
  waiting for transfers between devices  77.3 us (38%)
  Pallas kernels  25 us (12%)
  local copies, waits for them, and re-layouts  2.68 us (1%)
    ppermute x67, starting transfers between devices, route(): return lax.ppermute(value, ('section', 'head'), pairs)  93.1 us
    ppermute x67, waiting for transfers between devices, route(): return lax.ppermute(value, ('section', 'head'), pairs)  77.3 us
    pallas_call x4, Pallas kernels, on_device(): pl.pallas_call(functools.partial(layer_kernel, first, last, tick), out_sh...  18.1 us
  transfers between devices with their start and end apart: 67, of which 46 were waited for; matrix products, arithmetic and copies ran while one was open for 1% of the time, Pallas kernels for 5%

commit v1 on v0

--- a/solution.py
+++ b/solution.py
@@ -125,25 +125,23 @@
     return jnp.maximum(v, 0.0) + jnp.log1p(jnp.exp(-jnp.abs(v)))
 
 
-def fill_hidden(first, y, z, c, pieces, hidden):
+def fill_rows(first, y, z, c, pieces, gain_ref, rows, hidden):
     total = jnp.zeros((SLOTS, CELL), f32)
     for f in range(2):
         for e in range(4):
-            if first:
-                for d in range(4):
+            for d in range(4):
+                if first:
                     place = ((y ^ d) * 4 + (z ^ e)) * 2 + (c ^ f)
                     part = pieces[f][e, d]
-                    hidden[:, pl.ds(pl.multiple_of(place * CELL, CELL), CELL)] = part
-                    wide = part.astype(f32)
-                    total = total + wide * wide
-            else:
-                place = (c ^ f) * 4 + (z ^ e)
-                part = pieces[f][e]
-                hidden[:, pl.ds(pl.multiple_of(place * CHUNK, CHUNK), CHUNK)] = part
+                else:
+                    place = ((c ^ f) * 4 + (z ^ e)) * 4 + d
+                    part = pieces[f][e, :, d * CELL : (d + 1) * CELL]
+                at = pl.ds(pl.multiple_of(place * CELL, CELL), CELL)
                 wide = part.astype(f32)
-                square = wide * wide
-                for i in range(CHUNK // CELL):
-                    total = total + square[:, i * CELL : (i + 1) * CELL]
+                total = total + wide * wide
+                rows[:, at] = (wide * gain_ref[:, at]).astype(bf16)
+                if first:
+                    hidden[:, at] = part
     return jnp.sum(total, axis=1, keepdims=True)
 
 
@@ -151,6 +149,20 @@
     row = lax.broadcasted_iota(jnp.int32, (SHARE, SLOTS), 0)
     slot = lax.broadcasted_iota(jnp.int32, (SHARE, SLOTS), 1)
     return ((row < PACKED // 4) & (slot == section * (PACKED // 4) + row)).astype(bf16)
+
+
+def plan_kernel(accepted_ref, causal_ref, after_ref, batch_ref, owner_ref):
+    ends = ends_of(accepted_ref)
+    slots = (SLOTS, SLOTS)
+    row = lax.broadcasted_iota(jnp.int32, slots, 0)
+    column = lax.broadcasted_iota(jnp.int32, slots, 1)
+    same = owner_of(ends, row) == owner_of(ends, column)
+    causal_ref[...] = (same & (column <= row)).astype(f32)
+    after_ref[...] = (same & (column > row)).astype(f32)
+    batch = lax.broadcasted_iota(jnp.int32, (16, SLOTS), 0)
+    batch_owner = owner_of(ends, lax.broadcasted_iota(jnp.int32, (16, SLOTS), 1))
+    batch_ref[...] = (batch == batch_owner).astype(f32)
+    owner_ref[...] = owner_of(ends, lax.broadcasted_iota(jnp.int32, (SLOTS, STATE), 0))
 
 
 def project(last, gated, w_output, side, z, out_ref):
@@ -172,48 +184,50 @@
 
 
 def layer_kernel(first, last, tick, *refs):
-    (accepted_ref, bias_ref, rate_ref, skip_ref) = refs[:4]
-    pieces = refs[4:6]
-    (gain_ref, w_gate, w_input, w_pairs, w_step, w_output, states, place_ref) = refs[6:14]
-    refs = refs[14:]
+    (bias_ref, rate_ref, skip_ref) = refs[:3]
+    (causal_ref, after_ref, batch_ref, owner_ref) = refs[3:7]
+    pieces = refs[7:9]
+    (gain_ref, w_gate, w_input, w_pairs, w_step, w_output, states) = refs[9:16]
+    refs = refs[16:]
+    if first:
+        place_ref = refs[0]
+        refs = refs[1:]
     if not first:
         old_x, old_b, old_decay = refs[:3]
         refs = refs[3:]
     gated_ref, own_ref, sent_ref, new_x, new_b, new_decay = refs[:6]
-    hidden, normed = refs[-2:]
+    if first:
+        hidden = refs[-2]
+    else:
+        hidden = None
+    filled = refs[-1]
     x, y, z, c = coordinates()
-    ends = ends_of(accepted_ref)
-
-    squares = fill_hidden(first, y, z, c, pieces, hidden)
+
+    squares = fill_rows(first, y, z, c, pieces, gain_ref, filled, hidden)
     scale = lax.rsqrt(squares * (1.0 / WIDTH) + epsilon)
-    for i in range(WIDTH // CHUNK):
-        at = slice(i * CHUNK, (i + 1) * CHUNK)
-        normed[:, at] = (hidden[:, at].astype(f32) * scale * gain_ref[:, at]).astype(bf16)
-    rows = normed[...]
-    gate = jnp.dot(rows, w_gate[...], preferred_element_type=f32)
-    inner = jnp.dot(rows, w_input[...], preferred_element_type=f32)
-    pairs = lax.dot_general(rows, w_pairs[...], NT, preferred_element_type=f32).astype(bf16)
-    pairs = jnp.dot(pairs, place_ref[...], preferred_element_type=f32).astype(bf16)
+    rows = filled[...]
+    if first:
+        pairs = lax.dot_general(rows, w_pairs[...], NT, preferred_element_type=f32) * scale
+        pairs = jnp.dot(pairs.astype(bf16), place_ref[...], preferred_element_type=f32)
+    else:
+        pairs = jnp.dot(rows, w_pairs[...], preferred_element_type=f32) * scale
+    pairs = pairs.astype(bf16)
     b_vec, c_vec = pairs[:, :STATE], pairs[:, STATE:]
-    raw = lax.dot_general(rows, w_step[...], NT, preferred_element_type=f32)
-
-    lane = lax.broadcasted_iota(jnp.int32, (1, 16), 1)
-    bias = jnp.zeros((1, 16), f32)
-    rate = jnp.zeros((1, 16), f32)
+    raw = jnp.dot(rows, w_step[...], preferred_element_type=f32) * scale
+    inner = jnp.dot(rows, w_input[...], preferred_element_type=f32) * scale
+    gate = jnp.dot(rows, w_gate[...], preferred_element_type=f32) * scale
+
+    lane = lax.broadcasted_iota(jnp.int32, (1, CELL), 1)
+    bias = jnp.zeros((1, CELL), f32)
+    rate = jnp.zeros((1, CELL), f32)
     for h in range(4):
         bias = jnp.where(lane == h, bias_ref[0, h], bias)
         rate = jnp.where(lane == h, rate_ref[0, h], rate)
     step = softplus(raw + bias)
     fall = step * rate
 
-    row_owner = owner_of(ends, lax.broadcasted_iota(jnp.int32, (SLOTS, SLOTS), 0))
-    col_owner = owner_of(ends, lax.broadcasted_iota(jnp.int32, (SLOTS, SLOTS), 1))
-    same = row_owner == col_owner
-    ahead = lax.broadcasted_iota(jnp.int32, (SLOTS, SLOTS), 1) <= lax.broadcasted_iota(
-        jnp.int32, (SLOTS, SLOTS), 0
-    )
-    causal = same & ahead
-    causal_f32 = causal.astype(f32)
+    causal_f32 = causal_ref[...]
+    causal = causal_f32 > 0.0
     log_decay = -jnp.dot(
         causal_f32, fall, precision=lax.Precision.HIGHEST, preferred_element_type=f32
     )
@@ -224,19 +238,15 @@
         precision=lax.Precision.HIGHEST,
         preferred_element_type=f32,
     )
-    after = (same & jnp.logical_not(ahead)).astype(f32)
-    rest = -jnp.dot(after, fall, precision=lax.Precision.HIGHEST, preferred_element_type=f32)
-    batch = lax.broadcasted_iota(jnp.int32, (16, SLOTS), 0)
-    batch_owner = owner_of(ends, lax.broadcasted_iota(jnp.int32, (16, SLOTS), 1))
+    rest = -jnp.dot(
+        after_ref[...], fall, precision=lax.Precision.HIGHEST, preferred_element_type=f32
+    )
     total = -jnp.dot(
-        (batch == batch_owner).astype(f32),
-        fall,
-        precision=lax.Precision.HIGHEST,
-        preferred_element_type=f32,
+        batch_ref[...], fall, precision=lax.Precision.HIGHEST, preferred_element_type=f32
     )
 
     products = lax.dot_general(c_vec, b_vec, NT, preferred_element_type=f32)
-    slot_owner = owner_of(ends, lax.broadcasted_iota(jnp.int32, (SLOTS, STATE), 0))
+    slot_owner = owner_ref[...]
     carried = jnp.zeros((SLOTS, 4 * HEAD_DIM), f32)
     for b in range(ROWS):
         mine = jnp.where(slot_owner == b, c_vec, jnp.zeros((), bf16))
@@ -269,17 +279,20 @@
         weighted.append((jnp.exp(spread(rest, p)) * dx).astype(bf16))
     gated = jnp.concatenate(gated, axis=1)
 
-    half = WIDTH // 2
     if last:
         order = jnp.concatenate([share_rows(z ^ e) for e in range(4)], axis=0)
         gated = jnp.dot(order, gated, preferred_element_type=f32).astype(bf16)
-        own = hidden[:, pl.ds(pl.multiple_of(c * half, half), half)]
-        own = jnp.dot(order[:SHARE], own, preferred_element_type=f32).astype(bf16)
+        for k in range(4):
+            own = jnp.dot(order[:SHARE], pieces[0][z ^ k], preferred_element_type=f32)
+            own_ref[:, k * CHUNK : (k + 1) * CHUNK] = jnp.where(y == 0, own, 0.0).astype(bf16)
     else:
-        place = c * 4 + z
-        own = hidden[:, pl.ds(pl.multiple_of(place * CHUNK, CHUNK), CHUNK)]
+        if first:
+            place = c * 4 + z
+            own = hidden[:, pl.ds(pl.multiple_of(place * CHUNK, CHUNK), CHUNK)]
+        else:
+            own = pieces[0][0]
+        own_ref[...] = jnp.where(y == 0, own, jnp.zeros((), bf16))
     gated_ref[...] = gated
-    own_ref[...] = jnp.where(y == 0, own, jnp.zeros((), bf16))
     project(last, gated, w_output, c ^ 1, z, sent_ref)
 
     decay = jnp.exp(total)
@@ -298,9 +311,8 @@
         new_decay[...] = jnp.where(now, decay, old_decay[...])
 
 
-def state_kernel(accepted_ref, x_ref, b_ref, decay_ref, states, out_ref):
-    ends = ends_of(accepted_ref)
-    slot_owner = owner_of(ends, lax.broadcasted_iota(jnp.int32, (SLOTS, STATE), 0))
+def state_kernel(owner_ref, x_ref, b_ref, decay_ref, states, out_ref):
+    slot_owner = owner_ref[...]
     x_all = x_ref[...]
     b_all = b_ref[...]
     for b in range(ROWS):
@@ -426,7 +438,20 @@
     plane = jnp.stack([line] + [over_z(line, e) for e in (1, 2, 3)])
 
     pair_place = pair_places(y, z, c)
-    step_rows = jnp.pad(w_step[0].T, ((0, 12), (0, 0)))
+    step_columns = jnp.pad(w_step[0], ((0, 0), (0, CELL - 4)))
+    plan = pl.pallas_call(
+        plan_kernel,
+        out_shape=(
+            shape((SLOTS, SLOTS), f32),
+            shape((SLOTS, SLOTS), f32),
+            shape((16, SLOTS), f32),
+            shape((SLOTS, STATE), jnp.int32),
+        ),
+        in_specs=[SMEM],
+        out_specs=(VMEM,) * 4,
+        compiler_params=SMALL,
+        name="plan",
+    )(accepted)
     start_states = states[0].reshape(ROWS, 4 * HEAD_DIM, STATE)
     pieces = (plane, over_core(plane))
     w_pair = jnp.stack([w_merge, w_far])
@@ -434,7 +459,7 @@
     saved_kinds = (
         shape((SLOTS, 4 * HEAD_DIM), bf16),
         shape((SLOTS, STATE), bf16),
-        shape((16, 16), f32),
+        shape((16, CELL), f32),
     )
     saved = ()
     for tick in range(4):
@@ -447,32 +472,36 @@
         ) + saved_kinds
         if first:
             kinds = kinds + (shape((SHARE, WIDTH), bf16),)
+        extra = (pair_place,) if first else saved
         gated, own, sent, *saved = pl.pallas_call(
             functools.partial(layer_kernel, first, last, tick),
             out_shape=kinds,
-            in_specs=[SMEM] * 4 + [VMEM] * (10 + len(saved)),
+            in_specs=[SMEM] * 3 + [VMEM] * (13 + len(extra)),
             out_specs=(VMEM,) * len(kinds),
-            scratch_shapes=[pltpu.VMEM((SLOTS, WIDTH), bf16)] * 2,
+            scratch_shapes=[pltpu.VMEM((SLOTS, WIDTH), bf16)] * (2 if first else 1),
             compiler_params=PARAMS,
             name="layer",
         )(
-            accepted,
             step_bias,
             decay_rate,
             skip_gain,
+            *plan,
             *pieces,
             norm_gain,
             w_gate[0],
             w_input[0],
             w_pairs,
-            step_rows,
+            step_columns,
             w_output[0],
             start_states,
-            pair_place,
-            *saved,
+            *extra,
         )
         if first:
             tokens = saved.pop()
+            sent, w_pairs = lax.optimization_barrier((sent, w_pairs))
+            w_pairs = lax.dot_general(
+                w_pairs, pair_place, TN, preferred_element_type=f32
+            ).astype(bf16)
         kept = pl.pallas_call(
             functools.partial(keep_kernel, last),
             out_shape=shape(part, f32),
@@ -493,6 +522,8 @@
         for part in across:
             total = total + part.astype(f32)
         total = total.astype(bf16)
+        if first:
+            total, w_pairs = lax.optimization_barrier((total, w_pairs))
         if last:
             break
         arrived = [next_section(total, d) for d in range(4)]
@@ -509,11 +540,11 @@
     kept_states = pl.pallas_call(
         state_kernel,
         out_shape=shape((ROWS, 4 * HEAD_DIM, STATE), bf16),
-        in_specs=[SMEM] + [VMEM] * 4,
+        in_specs=[VMEM] * 5,
         out_specs=VMEM,
         compiler_params=SMALL,
         name="kept",
-    )(accepted, *saved, start_states)
+    )(plan[3], *saved, start_states)
 
     tokens_part = pl.pallas_call(
         tokens_kernel,

time: 201 us -> 199 us (0.990)
  Pallas kernels: 25 us -> 20.6 us
    pallas_call x4, Pallas kernels: 18.1 us -> 13.6 us  [on_device(): pl.pallas_call(functools.partial(layer_kernel, first, last, tick), out_sh...]
  transfers between devices with their start and end apart: 67 -> 67, of which waited for: 46 -> 46; matrix products, arithmetic and copies ran while one was open for 1% -> 2% of each run, Pallas kernels for 5% -> 4%
where the time goes in v1:
time: 199 us
  starting transfers between devices  93.1 us (47%)
  waiting for transfers between devices  77.3 us (39%)
  Pallas kernels  20.6 us (10%)
  local copies, waits for them, and re-layouts  3.38 us (2%)
  other arithmetic  2.11 us (1%)
    ppermute x67, starting transfers between devices, route(): return lax.ppermute(value, ('section', 'head'), pairs)  93.1 us
    ppermute x67, waiting for transfers between devices, route(): return lax.ppermute(value, ('section', 'head'), pairs)  77.3 us
    pallas_call x4, Pallas kernels, on_device(): pl.pallas_call(functools.partial(layer_kernel, first, last, tick), out_sh...  13.6 us
  transfers between devices with their start and end apart: 67, of which 46 were waited for; matrix products, arithmetic and copies ran while one was open for 2% of the time, Pallas kernels for 4%

profile of v1, /device:TPU:33, one launch (start us, length us, event | category | flops | bytes accessed | tf_op | source)
XLA Modules:
  0.0 198.8 jit_solution(16206634860335863239)
XLA Ops:
  0.7 2.6 %collective-permute-start.3 = (bf16[2048,128]{1,0:T(8,128)(2,1)}, bf16[2048,128]{1,0:T(8,128)(2,1)S(1)}, u32[]{:S(2)}, u32[]{:S(2)}) collective-permute-start(bf16[2048,128]{1,0:T(8,128)(2,1)} %refs_0_.11), channel_id=1, source_target_pairs={{0,96},{1,97},{2,98},{3,99},{4,100},{5,101},{6,102},{7,103},{8,104... | collective-permute-start | bytes 1572872 | tf_op jit(solution)/shard_map/ppermute | solution.py:40
  5.0 2.6 %collective-permute-start.1 = (bf16[16,4096]{1,0:T(8,128)(2,1)S(1)}, bf16[16,4096]{1,0:T(8,128)(2,1)S(1)}, u32[]{:S(2)}, u32[]{:S(2)}) collective-permute-start(bf16[16,4096]{1,0:T(8,128)(2,1)S(1)} %get-tuple-element.117), channel_id=1, source_target_pairs={{0,16},{1,17},{2,18},{3,19},{4,20},{5,21},{6,22},{7,23},{8,24},{9,... | collective-permute-start | bytes 393224 | tf_op jit(solution)/shard_map/ppermute | solution.py:40
  12.7 2.8 %collective-permute-done.2 = bf16[16,4096]{1,0:T(8,128)(2,1)S(1)} collective-permute-done((bf16[16,4096]{1,0:T(8,128)(2,1)S(1)}, bf16[16,4096]{1,0:T(8,128)(2,1)S(1)}, u32[]{:S(2)}, u32[]{:S(2)}) %collective-permute-start.2) | collective-permute-done | bytes 131104 | tf_op jit(solution)/shard_map/ppermute | solution.py:40
  18.9 2.7 %collective-permute-start.11 = (bf16[32,4096]{1,0:T(8,128)(2,1)}, bf16[32,4096]{1,0:T(8,128)(2,1)S(1)}, u32[]{:S(2)}, u32[]{:S(2)}) collective-permute-start(bf16[32,4096]{1,0:T(8,128)(2,1)} %pad_maximum_fusion.7), channel_id=1, source_target_pairs={{0,4},{1,5},{2,6},{3,7},{4,0},{5,1},{6,2},{7,3},{8,12},{9,13},{10,... | collective-permute-start | bytes 786440 | tf_op jit(solution)/shard_map/ppermute | solution.py:40
  21.7 2.7 %collective-permute-start.9 = (bf16[80,128]{1,0:T(8,128)(2,1)S(1)}, bf16[80,128]{1,0:T(8,128)(2,1)S(1)}, u32[]{:S(2)}, u32[]{:S(2)}) collective-permute-start(bf16[80,128]{1,0:T(8,128)(2,1)S(1)} %add_convert_fusion.4), channel_id=1, source_target_pairs={{0,24},{1,25},{2,26},{3,27},{4,28},{5,29},{6,30},{7,31},{8,16},{9,... | collective-permute-start | bytes 61448 | tf_op jit(solution)/shard_map/ppermute | solution.py:40
  29.8 3.0 %collective-permute-done.10 = bf16[32,4096]{1,0:T(8,128)(2,1)S(1)} collective-permute-done((bf16[32,4096]{1,0:T(8,128)(2,1)S(1)}, bf16[32,4096]{1,0:T(8,128)(2,1)S(1)}, u32[]{:S(2)}, u32[]{:S(2)}) %collective-permute-start.10) | collective-permute-done | bytes 262176 | tf_op jit(solution)/shard_map/ppermute | solution.py:40
  44.6 4.4 %layer.4 = (bf16[80,256]{1,0:T(8,128)(2,1)S(1)}, bf16[80,512]{1,0:T(8,128)(2,1)S(1)}, bf16[4,80,512]{2,1,0:T(8,128)(2,1)S(1)}, bf16[80,256]{1,0:T(8,128)(2,1)S(1...) custom-call(f32[1,4]{1,0:T(1,128)S(1)} %copy-done.9, f32[1,4]{1,0:T(1,128)S(1)} %copy-done.10, ...), custom_call_target="tpu_custom_call" | custom-call | tf_op jit(solution)/shard_map/layer/pallas_call | solution.py:476
  52.5 2.3 %collective-permute-start.20 = (bf16[80,512]{1,0:T(8,128)(2,1)S(1)}, bf16[80,512]{1,0:T(8,128)(2,1)S(1)}, u32[]{:S(2)}, u32[]{:S(2)}) collective-permute-start(bf16[80,512]{1,0:T(8,128)(2,1)S(1)} %get-tuple-element.131), channel_id=1, source_target_pairs={{0,4},{1,5},{2,6},{3,7},{4,0},{5,1},{6,2},{7,3},{8,12},{9,13},{10,... | collective-permute-start | bytes 245768 | tf_op jit(solution)/shard_map/ppermute | solution.py:40
  58.5 3.3 %collective-permute-start.25 = (bf16[80,512]{1,0:T(8,128)(2,1)S(1)}, bf16[80,512]{1,0:T(8,128)(2,1)S(1)}, u32[]{:S(2)}, u32[]{:S(2)}) collective-permute-start(bf16[80,512]{1,0:T(8,128)(2,1)S(1)} %fusion.17), channel_id=1, source_target_pairs={{0,56},{1,57},{2,58},{3,59},{4,60},{5,61},{6,62},{7,63},{8,48},{9,... | collective-permute-start | bytes 245768 | tf_op jit(solution)/shard_map/ppermute | solution.py:40
  65.2 3.5 %collective-permute-done.24 = bf16[80,512]{1,0:T(8,128)(2,1)S(1)} collective-permute-done((bf16[80,512]{1,0:T(8,128)(2,1)S(1)}, bf16[80,512]{1,0:T(8,128)(2,1)S(1)}, u32[]{:S(2)}, u32[]{:S(2)}) %collective-permute-start.24) | collective-permute-done | bytes 81952 | tf_op jit(solution)/shard_map/ppermute | solution.py:40
  74.2 2.7 %collective-permute-done.27 = bf16[80,512]{1,0:T(8,128)(2,1)S(1)} collective-permute-done((bf16[80,512]{1,0:T(8,128)(2,1)S(1)}, bf16[80,512]{1,0:T(8,128)(2,1)S(1)}, u32[]{:S(2)}, u32[]{:S(2)}) %collective-permute-start.27) | collective-permute-done | bytes 81952 | tf_op jit(solution)/shard_map/ppermute | solution.py:40
  77.7 3.3 %collective-permute-start.29 = (bf16[4,80,512]{2,1,0:T(8,128)(2,1)S(1)}, bf16[4,80,512]{2,1,0:T(8,128)(2,1)S(1)}, u32[]{:S(2)}, u32[]{:S(2)}) collective-permute-start(bf16[4,80,512]{2,1,0:T(8,128)(2,1)S(1)} %pad_maximum_fusion.3.refs_7_), channel_id=1, source_target_pairs={{0,1},{1,0},{2,3},{3,2},{4,5},{5,4},{6,7},{7,6},{8,9},{9,8},{10,11... | collective-permute-start | bytes 983048 | tf_op jit(solution)/shard_map/ppermute | solution.py:40
  82.2 3.0 %layer.5 = (bf16[80,256]{1,0:T(8,128)(2,1)S(1)}, bf16[80,512]{1,0:T(8,128)(2,1)S(1)}, bf16[4,80,512]{2,1,0:T(8,128)(2,1)S(1)}, bf16[80,256]{1,0:T(8,128)(2,1)S(1...) custom-call(f32[1,4]{1,0:T(1,128)S(1)} %copy-done.9, f32[1,4]{1,0:T(1,128)S(1)} %copy-done.10, ...), custom_call_target="tpu_custom_call" | custom-call | tf_op jit(solution)/shard_map/layer/pallas_call | solution.py:476
  101.0 2.5 %collective-permute-done.36 = bf16[80,512]{1,0:T(8,128)(2,1)S(1)} collective-permute-done((bf16[80,512]{1,0:T(8,128)(2,1)S(1)}, bf16[80,512]{1,0:T(8,128)(2,1)S(1)}, u32[]{:S(2)}, u32[]{:S(2)}) %collective-permute-start.36) | collective-permute-done | bytes 81952 | tf_op jit(solution)/shard_map/ppermute | solution.py:40
  111.5 4.0 %collective-permute-start.41 = (bf16[4,80,512]{2,1,0:T(8,128)(2,1)S(1)}, bf16[4,80,512]{2,1,0:T(8,128)(2,1)S(1)}, u32[]{:S(2)}, u32[]{:S(2)}) collective-permute-start(bf16[4,80,512]{2,1,0:T(8,128)(2,1)S(1)} %pad_maximum_fusion.4.refs_7_), channel_id=1, source_target_pairs={{0,1},{1,0},{2,3},{3,2},{4,5},{5,4},{6,7},{7,6},{8,9},{9,8},{10,11... | collective-permute-start | bytes 983048 | tf_op jit(solution)/shard_map/ppermute | solution.py:40
  116.8 3.0 %layer.6 = (bf16[80,256]{1,0:T(8,128)(2,1)S(1)}, bf16[80,512]{1,0:T(8,128)(2,1)S(1)}, bf16[4,80,512]{2,1,0:T(8,128)(2,1)S(1)}, bf16[80,256]{1,0:T(8,128)(2,1)S(1...) custom-call(f32[1,4]{1,0:T(1,128)S(1)} %copy-done.9, f32[1,4]{1,0:T(1,128)S(1)} %copy-done.10, ...), custom_call_target="tpu_custom_call" | custom-call | tf_op jit(solution)/shard_map/layer/pallas_call | solution.py:476
  132.4 2.2 %collective-permute-start.46 = (bf16[80,512]{1,0:T(8,128)(2,1)S(1)}, bf16[80,512]{1,0:T(8,128)(2,1)S(1)}, u32[]{:S(2)}, u32[]{:S(2)}) collective-permute-start(bf16[80,512]{1,0:T(8,128)(2,1)S(1)} %fusion.9), channel_id=1, source_target_pairs={{0,32},{1,33},{2,34},{3,35},{4,36},{5,37},{6,38},{7,39},{8,40},{9,... | collective-permute-start | bytes 245768 | tf_op jit(solution)/shard_map/ppermute | solution.py:40
  135.4 2.6 %collective-permute-done.48 = bf16[80,512]{1,0:T(8,128)(2,1)S(1)} collective-permute-done((bf16[80,512]{1,0:T(8,128)(2,1)S(1)}, bf16[80,512]{1,0:T(8,128)(2,1)S(1)}, u32[]{:S(2)}, u32[]{:S(2)}) %collective-permute-start.48) | collective-permute-done | bytes 81952 | tf_op jit(solution)/shard_map/ppermute | solution.py:40
  142.6 2.3 %collective-permute-done.51 = bf16[80,512]{1,0:T(8,128)(2,1)S(1)} collective-permute-done((bf16[80,512]{1,0:T(8,128)(2,1)S(1)}, bf16[80,512]{1,0:T(8,128)(2,1)S(1)}, u32[]{:S(2)}, u32[]{:S(2)}) %collective-permute-start.51) | collective-permute-done | bytes 81952 | tf_op jit(solution)/shard_map/ppermute | solution.py:40
  145.6 4.2 %collective-permute-start.53 = (bf16[4,80,512]{2,1,0:T(8,128)(2,1)S(1)}, bf16[4,80,512]{2,1,0:T(8,128)(2,1)S(1)}, u32[]{:S(2)}, u32[]{:S(2)}) collective-permute-start(bf16[4,80,512]{2,1,0:T(8,128)(2,1)S(1)} %pad_maximum_fusion.5.refs_7_), channel_id=1, source_target_pairs={{0,1},{1,0},{2,3},{3,2},{4,5},{5,4},{6,7},{7,6},{8,9},{9,8},{10,11... | collective-permute-start | bytes 983048 | tf_op jit(solution)/shard_map/ppermute | solution.py:40
  151.0 3.2 %layer.7 = (bf16[96,256]{1,0:T(8,128)(2,1)S(1)}, bf16[24,2048]{1,0:T(8,128)(2,1)S(1)}, bf16[4,24,2048]{2,1,0:T(8,128)(2,1)S(1)}, bf16[80,256]{1,0:T(8,128)(2,1)S...) custom-call(f32[1,4]{1,0:T(1,128)S(1)} %copy-done.9, f32[1,4]{1,0:T(1,128)S(1)} %copy-done.10, ...), custom_call_target="tpu_custom_call" | custom-call | tf_op jit(solution)/shard_map/layer/pallas_call | solution.py:476
  156.0 5.9 %collective-permute-done.55.refs_2_ = bf16[2,2048,128]{2,1,0:T(8,128)(2,1)S(1)} collective-permute-done((bf16[2,2048,128]{2,1,0:T(8,128)(2,1)S(1)}, bf16[2,2048,128]{2,1,0:T(8,128)(2,1)S(1)}, u32[]{:S(2)}, u32[]{:S(2)}) %collective-permute-start.55) | collective-permute-done | bytes 1048608 | tf_op jit(solution)/shard_map/ppermute | solution.py:40
  180.2 9.7 %collective-permute-done.63 = bf16[24,2048]{1,0:T(8,128)(2,1)S(1)} collective-permute-done((bf16[24,2048]{1,0:T(8,128)(2,1)S(1)}, bf16[24,2048]{1,0:T(8,128)(2,1)S(1)}, u32[]{:S(2)}, u32[]{:S(2)}) %collective-permute-start.63) | collective-permute-done | bytes 98336 | tf_op jit(solution)/shard_map/ppermute | solution.py:40
  189.9 6.8 %collective-permute-start.66 = (bf16[24,2048]{1,0:T(8,128)(2,1)S(1)}, bf16[24,2048]{1,0:T(8,128)(2,1)S(1)}, u32[]{:S(2)}, u32[]{:S(2)}) collective-permute-start(bf16[24,2048]{1,0:T(8,128)(2,1)S(1)} %add_add_fusion.own_ref), channel_id=1, source_target_pairs={{0,1},{1,0},{2,3},{3,2},{4,5},{5,4},{6,7},{7,6},{8,9},{9,8},{10,11... | collective-permute-start | bytes 294920 | tf_op jit(solution)/shard_map/ppermute | solution.py:40
  (196 shorter events, 112.4 us)
Async XLA Ops:
  0.7 14.8 %collective-permute-start.3 = (bf16[2048,128]{1,0:T(8,128)(2,1)}, bf16[2048,128]{1,0:T(8,128)(2,1)S(1)}, u32[]{:S(2)}, u32[]{:S(2)}) collective-permute-start(bf16[2048,128]{1,0:T(8,128)(2,1)} %refs_0_.11), channel_id=1, source_target_pairs={{0,96},{1,97},{2,98},{3,99},{4,100},{5,101},{6,102},{7,103},{8,104... | collective-permute-start | bytes 1572872 | tf_op jit(solution)/shard_map/ppermute | solution.py:40
  3.6 8.6 %collective-permute-start = (bf16[16,4096]{1,0:T(8,128)(2,1)S(1)}, bf16[16,4096]{1,0:T(8,128)(2,1)S(1)}, u32[]{:S(2)}, u32[]{:S(2)}) collective-permute-start(bf16[16,4096]{1,0:T(8,128)(2,1)S(1)} %get-tuple-element.118), channel_id=1, source_target_pairs={{0,8},{1,9},{2,10},{3,11},{4,12},{5,13},{6,14},{7,15},{8,0},{9,1},... | collective-permute-start | bytes 393224 | tf_op jit(solution)/shard_map/ppermute | solution.py:40
  5.0 7.7 %collective-permute-start.1 = (bf16[16,4096]{1,0:T(8,128)(2,1)S(1)}, bf16[16,4096]{1,0:T(8,128)(2,1)S(1)}, u32[]{:S(2)}, u32[]{:S(2)}) collective-permute-start(bf16[16,4096]{1,0:T(8,128)(2,1)S(1)} %get-tuple-element.117), channel_id=1, source_target_pairs={{0,16},{1,17},{2,18},{3,19},{4,20},{5,21},{6,22},{7,23},{8,24},{9,... | collective-permute-start | bytes 393224 | tf_op jit(solution)/shard_map/ppermute | solution.py:40
  7.6 7.9 %collective-permute-start.2 = (bf16[16,4096]{1,0:T(8,128)(2,1)S(1)}, bf16[16,4096]{1,0:T(8,128)(2,1)S(1)}, u32[]{:S(2)}, u32[]{:S(2)}) collective-permute-start(bf16[16,4096]{1,0:T(8,128)(2,1)S(1)} %get-tuple-element.116), channel_id=1, source_target_pairs={{0,24},{1,25},{2,26},{3,27},{4,28},{5,29},{6,30},{7,31},{8,16},{9,... | collective-permute-start | bytes 393224 | tf_op jit(solution)/shard_map/ppermute | solution.py:40
  15.5 6.1 %collective-permute-start.6 = (bf16[80,128]{1,0:T(8,128)(2,1)S(1)}, bf16[80,128]{1,0:T(8,128)(2,1)S(1)}, u32[]{:S(2)}, u32[]{:S(2)}) collective-permute-start(bf16[80,128]{1,0:T(8,128)(2,1)S(1)} %look.1), channel_id=1, source_target_pairs={{0,64},{1,65},{2,66},{3,67},{4,68},{5,69},{6,70},{7,71},{8,72},{9,... | collective-permute-start | bytes 61448 | tf_op jit(solution)/shard_map/ppermute | solution.py:40
  18.9 13.8 %collective-permute-start.11 = (bf16[32,4096]{1,0:T(8,128)(2,1)}, bf16[32,4096]{1,0:T(8,128)(2,1)S(1)}, u32[]{:S(2)}, u32[]{:S(2)}) collective-permute-start(bf16[32,4096]{1,0:T(8,128)(2,1)} %pad_maximum_fusion.7), channel_id=1, source_target_pairs={{0,4},{1,5},{2,6},{3,7},{4,0},{5,1},{6,2},{7,3},{8,12},{9,13},{10,... | collective-permute-start | bytes 786440 | tf_op jit(solution)/shard_map/ppermute | solution.py:40
  21.6 12.9 %collective-permute-start.12 = (bf16[32,4096]{1,0:T(8,128)(2,1)}, bf16[32,4096]{1,0:T(8,128)(2,1)S(1)}, u32[]{:S(2)}, u32[]{:S(2)}) collective-permute-start(bf16[32,4096]{1,0:T(8,128)(2,1)} %pad_maximum_fusion.7), channel_id=1, source_target_pairs={{0,6},{1,7},{2,4},{3,5},{4,2},{5,3},{6,0},{7,1},{8,14},{9,15},{10,... | collective-permute-start | bytes 786440 | tf_op jit(solution)/shard_map/ppermute | solution.py:40
  24.4 8.4 %collective-permute-start.10 = (bf16[32,4096]{1,0:T(8,128)(2,1)S(1)}, bf16[32,4096]{1,0:T(8,128)(2,1)S(1)}, u32[]{:S(2)}, u32[]{:S(2)}) collective-permute-start(bf16[32,4096]{1,0:T(8,128)(2,1)S(1)} %pad_maximum_fusion.6), channel_id=1, source_target_pairs={{0,2},{1,3},{2,0},{3,1},{4,6},{5,7},{6,4},{7,5},{8,10},{9,11},{10,... | collective-permute-start | bytes 786440 | tf_op jit(solution)/shard_map/ppermute | solution.py:40
  58.5 6.7 %collective-permute-start.25 = (bf16[80,512]{1,0:T(8,128)(2,1)S(1)}, bf16[80,512]{1,0:T(8,128)(2,1)S(1)}, u32[]{:S(2)}, u32[]{:S(2)}) collective-permute-start(bf16[80,512]{1,0:T(8,128)(2,1)S(1)} %fusion.17), channel_id=1, source_target_pairs={{0,56},{1,57},{2,58},{3,59},{4,60},{5,61},{6,62},{7,63},{8,48},{9,... | collective-permute-start | bytes 245768 | tf_op jit(solution)/shard_map/ppermute | solution.py:40
  61.8 6.9 %collective-permute-start.24 = (bf16[80,512]{1,0:T(8,128)(2,1)S(1)}, bf16[80,512]{1,0:T(8,128)(2,1)S(1)}, u32[]{:S(2)}, u32[]{:S(2)}) collective-permute-start(bf16[80,512]{1,0:T(8,128)(2,1)S(1)} %fusion.17), channel_id=1, source_target_pairs={{0,48},{1,49},{2,50},{3,51},{4,52},{5,53},{6,54},{7,55},{8,56},{9,... | collective-permute-start | bytes 245768 | tf_op jit(solution)/shard_map/ppermute | solution.py:40
  62.9 5.8 %collective-permute-start.23 = (bf16[80,512]{1,0:T(8,128)(2,1)S(1)}, bf16[80,512]{1,0:T(8,128)(2,1)S(1)}, u32[]{:S(2)}, u32[]{:S(2)}) collective-permute-start(bf16[80,512]{1,0:T(8,128)(2,1)S(1)} %fusion.17), channel_id=1, source_target_pairs={{0,40},{1,41},{2,42},{3,43},{4,44},{5,45},{6,46},{7,47},{8,32},{9,... | collective-permute-start | bytes 245768 | tf_op jit(solution)/shard_map/ppermute | solution.py:40
  63.8 7.1 %collective-permute-start.22 = (bf16[80,512]{1,0:T(8,128)(2,1)S(1)}, bf16[80,512]{1,0:T(8,128)(2,1)S(1)}, u32[]{:S(2)}, u32[]{:S(2)}) collective-permute-start(bf16[80,512]{1,0:T(8,128)(2,1)S(1)} %fusion.17), channel_id=1, source_target_pairs={{0,32},{1,33},{2,34},{3,35},{4,36},{5,37},{6,38},{7,39},{8,40},{9,... | collective-permute-start | bytes 245768 | tf_op jit(solution)/shard_map/ppermute | solution.py:40
  94.3 6.7 %collective-permute-start.37 = (bf16[80,512]{1,0:T(8,128)(2,1)S(1)}, bf16[80,512]{1,0:T(8,128)(2,1)S(1)}, u32[]{:S(2)}, u32[]{:S(2)}) collective-permute-start(bf16[80,512]{1,0:T(8,128)(2,1)S(1)} %fusion.13), channel_id=1, source_target_pairs={{0,56},{1,57},{2,58},{3,59},{4,60},{5,61},{6,62},{7,63},{8,48},{9,... | collective-permute-start | bytes 245768 | tf_op jit(solution)/shard_map/ppermute | solution.py:40
  95.6 7.9 %collective-permute-start.36 = (bf16[80,512]{1,0:T(8,128)(2,1)S(1)}, bf16[80,512]{1,0:T(8,128)(2,1)S(1)}, u32[]{:S(2)}, u32[]{:S(2)}) collective-permute-start(bf16[80,512]{1,0:T(8,128)(2,1)S(1)} %fusion.13), channel_id=1, source_target_pairs={{0,48},{1,49},{2,50},{3,51},{4,52},{5,53},{6,54},{7,55},{8,56},{9,... | collective-permute-start | bytes 245768 | tf_op jit(solution)/shard_map/ppermute | solution.py:40
  96.5 7.0 %collective-permute-start.35 = (bf16[80,512]{1,0:T(8,128)(2,1)S(1)}, bf16[80,512]{1,0:T(8,128)(2,1)S(1)}, u32[]{:S(2)}, u32[]{:S(2)}) collective-permute-start(bf16[80,512]{1,0:T(8,128)(2,1)S(1)} %fusion.13), channel_id=1, source_target_pairs={{0,40},{1,41},{2,42},{3,43},{4,44},{5,45},{6,46},{7,47},{8,32},{9,... | collective-permute-start | bytes 245768 | tf_op jit(solution)/shard_map/ppermute | solution.py:40
  98.2 6.9 %collective-permute-start.34 = (bf16[80,512]{1,0:T(8,128)(2,1)S(1)}, bf16[80,512]{1,0:T(8,128)(2,1)S(1)}, u32[]{:S(2)}, u32[]{:S(2)}) collective-permute-start(bf16[80,512]{1,0:T(8,128)(2,1)S(1)} %fusion.13), channel_id=1, source_target_pairs={{0,32},{1,33},{2,34},{3,35},{4,36},{5,37},{6,38},{7,39},{8,40},{9,... | collective-permute-start | bytes 245768 | tf_op jit(solution)/shard_map/ppermute | solution.py:40
  128.7 6.7 %collective-permute-start.49 = (bf16[80,512]{1,0:T(8,128)(2,1)S(1)}, bf16[80,512]{1,0:T(8,128)(2,1)S(1)}, u32[]{:S(2)}, u32[]{:S(2)}) collective-permute-start(bf16[80,512]{1,0:T(8,128)(2,1)S(1)} %fusion.9), channel_id=1, source_target_pairs={{0,56},{1,57},{2,58},{3,59},{4,60},{5,61},{6,62},{7,63},{8,48},{9,... | collective-permute-start | bytes 245768 | tf_op jit(solution)/shard_map/ppermute | solution.py:40
  130.3 7.7 %collective-permute-start.48 = (bf16[80,512]{1,0:T(8,128)(2,1)S(1)}, bf16[80,512]{1,0:T(8,128)(2,1)S(1)}, u32[]{:S(2)}, u32[]{:S(2)}) collective-permute-start(bf16[80,512]{1,0:T(8,128)(2,1)S(1)} %fusion.9), channel_id=1, source_target_pairs={{0,48},{1,49},{2,50},{3,51},{4,52},{5,53},{6,54},{7,55},{8,56},{9,... | collective-permute-start | bytes 245768 | tf_op jit(solution)/shard_map/ppermute | solution.py:40
  130.9 7.1 %collective-permute-start.47 = (bf16[80,512]{1,0:T(8,128)(2,1)S(1)}, bf16[80,512]{1,0:T(8,128)(2,1)S(1)}, u32[]{:S(2)}, u32[]{:S(2)}) collective-permute-start(bf16[80,512]{1,0:T(8,128)(2,1)S(1)} %fusion.9), channel_id=1, source_target_pairs={{0,40},{1,41},{2,42},{3,43},{4,44},{5,45},{6,46},{7,47},{8,32},{9,... | collective-permute-start | bytes 245768 | tf_op jit(solution)/shard_map/ppermute | solution.py:40
  132.4 6.6 %collective-permute-start.46 = (bf16[80,512]{1,0:T(8,128)(2,1)S(1)}, bf16[80,512]{1,0:T(8,128)(2,1)S(1)}, u32[]{:S(2)}, u32[]{:S(2)}) collective-permute-start(bf16[80,512]{1,0:T(8,128)(2,1)S(1)} %fusion.9), channel_id=1, source_target_pairs={{0,32},{1,33},{2,34},{3,35},{4,36},{5,37},{6,38},{7,39},{8,40},{9,... | collective-permute-start | bytes 245768 | tf_op jit(solution)/shard_map/ppermute | solution.py:40
  139.1 22.8 %collective-permute-start.55 = (bf16[2,2048,128]{2,1,0:T(8,128)(2,1)S(1)}, bf16[2,2048,128]{2,1,0:T(8,128)(2,1)S(1)}, u32[]{:S(2)}, u32[]{:S(2)}) collective-permute-start(bf16[2,2048,128]{2,1,0:T(8,128)(2,1)S(1)} %pad_maximum_fusion.1), channel_id=1, source_target_pairs={{0,32},{1,33},{2,34},{3,35},{4,36},{5,37},{6,38},{7,39},{8,40},{9,... | collective-permute-start | bytes 3145736 | tf_op jit(solution)/shard_map/ppermute | solution.py:40
  168.8 5.6 %collective-permute-start.59 = (bf16[24,2048]{1,0:T(8,128)(2,1)S(1)}, bf16[24,2048]{1,0:T(8,128)(2,1)S(1)}, u32[]{:S(2)}, u32[]{:S(2)}) collective-permute-start(bf16[24,2048]{1,0:T(8,128)(2,1)S(1)} %fusion.5), channel_id=1, source_target_pairs={{0,8},{1,9},{2,10},{3,11},{4,12},{5,13},{6,14},{7,15},{8,0},{9,1},... | collective-permute-start | bytes 294920 | tf_op jit(solution)/shard_map/ppermute | solution.py:40
  178.9 11.1 %collective-permute-start.63 = (bf16[24,2048]{1,0:T(8,128)(2,1)S(1)}, bf16[24,2048]{1,0:T(8,128)(2,1)S(1)}, u32[]{:S(2)}, u32[]{:S(2)}) collective-permute-start(bf16[24,2048]{1,0:T(8,128)(2,1)S(1)} %add_convert_fusion), channel_id=1, source_target_pairs={{96,2},{97,3},{98,32},{99,33},{100,70},{101,71},{102,100},{103,101... | collective-permute-start | bytes 294920 | tf_op jit(solution)/shard_map/ppermute | solution.py:40
  189.9 7.7 %collective-permute-start.66 = (bf16[24,2048]{1,0:T(8,128)(2,1)S(1)}, bf16[24,2048]{1,0:T(8,128)(2,1)S(1)}, u32[]{:S(2)}, u32[]{:S(2)}) collective-permute-start(bf16[24,2048]{1,0:T(8,128)(2,1)S(1)} %add_add_fusion.own_ref), channel_id=1, source_target_pairs={{0,1},{1,0},{2,3},{3,2},{4,5},{5,4},{6,7},{7,6},{8,9},{9,8},{10,11... | collective-permute-start | bytes 294920 | tf_op jit(solution)/shard_map/ppermute | solution.py:40
  (58 other events, 303.0 us)

commit v2 on v1

--- a/solution.py
+++ b/solution.py
@@ -14,7 +14,7 @@
 POS = 5
 ROWS = 12
 PACKED = 2 * ACCEPTED
-SLOTS = 80
+SLOTS = 72
 WIDTH = 4096
 CHUNK = 512
 CELL = 128
@@ -148,7 +148,7 @@
 def share_rows(section):
     row = lax.broadcasted_iota(jnp.int32, (SHARE, SLOTS), 0)
     slot = lax.broadcasted_iota(jnp.int32, (SHARE, SLOTS), 1)
-    return ((row < PACKED // 4) & (slot == section * (PACKED // 4) + row)).astype(bf16)
+    return ((row < PACKED // 4) & (slot == section * (PACKED // 4) + row)).astype(f32)
 
 
 def plan_kernel(accepted_ref, causal_ref, after_ref, batch_ref, owner_ref):
@@ -169,12 +169,13 @@
     for e in range(4):
         place = side * 4 + (e if last else z ^ e)
         w = w_output[:, pl.ds(pl.multiple_of(place * CHUNK, CHUNK), CHUNK)]
-        part = jnp.dot(gated, w, preferred_element_type=f32).astype(out_ref.dtype)
+        part = jnp.dot(gated, w, preferred_element_type=f32)
         if last:
             for g in range(4):
-                out_ref[g, :, e * CHUNK : (e + 1) * CHUNK] = part[g * SHARE : (g + 1) * SHARE]
+                group = part[g * SHARE : (g + 1) * SHARE].astype(out_ref.dtype)
+                out_ref[g, :, e * CHUNK : (e + 1) * CHUNK] = group
         else:
-            out_ref[e] = part
+            out_ref[e] = part.astype(out_ref.dtype)
 
 
 def keep_kernel(last, gated_ref, own_ref, w_output, out_ref):
@@ -280,10 +281,11 @@
     gated = jnp.concatenate(gated, axis=1)
 
     if last:
-        order = jnp.concatenate([share_rows(z ^ e) for e in range(4)], axis=0)
+        order = jnp.concatenate([share_rows(z ^ e) for e in range(4)], axis=0).astype(bf16)
+        share = share_rows(z).astype(bf16)
         gated = jnp.dot(order, gated, preferred_element_type=f32).astype(bf16)
         for k in range(4):
-            own = jnp.dot(order[:SHARE], pieces[0][z ^ k], preferred_element_type=f32)
+            own = jnp.dot(share, pieces[0][z ^ k], preferred_element_type=f32)
             own_ref[:, k * CHUNK : (k + 1) * CHUNK] = jnp.where(y == 0, own, 0.0).astype(bf16)
     else:
         if first:
@@ -297,7 +299,7 @@
 
     decay = jnp.exp(total)
     if first:
-        share = share_rows(x)
+        share = share_rows(x).astype(bf16)
         refs[6][...] = jnp.dot(share, hidden[...], preferred_element_type=f32).astype(bf16)
         new_x[:, :128] = weighted[0]
         new_x[:, 128:] = weighted[1]

time: 199 us -> 197 us (0.990)
  waiting for transfers between devices: 77.3 us -> 73.1 us
    ppermute x67, waiting for transfers between devices: 77.3 us -> 73.1 us  [route(): return lax.ppermute(value, ('section', 'head'), pairs)]
  transfers between devices with their start and end apart: 67 -> 67, of which waited for: 46 -> 43; matrix products, arithmetic and copies ran while one was open for 2% -> 2% of each run, Pallas kernels for 4% -> 4%
where the time goes in v2:
time: 197 us
  starting transfers between devices  94.8 us (48%)
  waiting for transfers between devices  73.1 us (37%)
  Pallas kernels  20.8 us (11%)
  local copies, waits for them, and re-layouts  3.45 us (2%)
  other arithmetic  2.04 us (1%)
    ppermute x67, starting transfers between devices, route(): return lax.ppermute(value, ('section', 'head'), pairs)  94.8 us
    ppermute x67, waiting for transfers between devices, route(): return lax.ppermute(value, ('section', 'head'), pairs)  73.1 us
    pallas_call x4, Pallas kernels, on_device(): pl.pallas_call(functools.partial(layer_kernel, first, last, tick), out_sh...  13.9 us
  transfers between devices with their start and end apart: 67, of which 43 were waited for; matrix products, arithmetic and copies ran while one was open for 2% of the time, Pallas kernels for 4%

profile of v2, /device:TPU:33, one launch (start us, length us, event | category | flops | bytes accessed | tf_op | source)
XLA Modules:
  0.0 196.6 jit_solution(11306889465017823729)
XLA Ops:
  0.7 2.6 %collective-permute-start.3 = (bf16[2048,128]{1,0:T(8,128)(2,1)}, bf16[2048,128]{1,0:T(8,128)(2,1)S(1)}, u32[]{:S(2)}, u32[]{:S(2)}) collective-permute-start(bf16[2048,128]{1,0:T(8,128)(2,1)} %refs_0_.11), channel_id=1, source_target_pairs={{0,96},{1,97},{2,98},{3,99},{4,100},{5,101},{6,102},{7,103},{8,104... | collective-permute-start | bytes 1572872 | tf_op jit(solution)/shard_map/ppermute | solution.py:40
  5.0 2.6 %collective-permute-start.1 = (bf16[16,4096]{1,0:T(8,128)(2,1)S(1)}, bf16[16,4096]{1,0:T(8,128)(2,1)S(1)}, u32[]{:S(2)}, u32[]{:S(2)}) collective-permute-start(bf16[16,4096]{1,0:T(8,128)(2,1)S(1)} %get-tuple-element.117), channel_id=1, source_target_pairs={{0,16},{1,17},{2,18},{3,19},{4,20},{5,21},{6,22},{7,23},{8,24},{9,... | collective-permute-start | bytes 393224 | tf_op jit(solution)/shard_map/ppermute | solution.py:40
  9.9 2.2 %look.1 = bf16[72,128]{1,0:T(8,128)(2,1)S(1)} custom-call(s32[2,12]{1,0:T(2,128)S(1)} %copy-done.12, s32[2,12,5]{2,1,0:T(8,128)S(1)} %copy.17.tokens_ref, bf16[16384,128]{1,0:T(8,128)(2,1)S(1)} %copy-done.6), custom_call_target="tpu_custom_call" | custom-call | flops 1000000000 | bytes 10000000 | tf_op jit(solution)/shard_map/look/pallas_call | solution.py:413
  12.7 2.8 %collective-permute-done.2 = bf16[16,4096]{1,0:T(8,128)(2,1)S(1)} collective-permute-done((bf16[16,4096]{1,0:T(8,128)(2,1)S(1)}, bf16[16,4096]{1,0:T(8,128)(2,1)S(1)}, u32[]{:S(2)}, u32[]{:S(2)}) %collective-permute-start.2) | collective-permute-done | bytes 131104 | tf_op jit(solution)/shard_map/ppermute | solution.py:40
  18.9 2.7 %collective-permute-start.11 = (bf16[32,4096]{1,0:T(8,128)(2,1)}, bf16[32,4096]{1,0:T(8,128)(2,1)S(1)}, u32[]{:S(2)}, u32[]{:S(2)}) collective-permute-start(bf16[32,4096]{1,0:T(8,128)(2,1)} %pad_maximum_fusion.7), channel_id=1, source_target_pairs={{0,4},{1,5},{2,6},{3,7},{4,0},{5,1},{6,2},{7,3},{8,12},{9,13},{10,... | collective-permute-start | bytes 786440 | tf_op jit(solution)/shard_map/ppermute | solution.py:40
  21.7 2.7 %collective-permute-start.9 = (bf16[72,128]{1,0:T(8,128)(2,1)S(1)}, bf16[72,128]{1,0:T(8,128)(2,1)S(1)}, u32[]{:S(2)}, u32[]{:S(2)}) collective-permute-start(bf16[72,128]{1,0:T(8,128)(2,1)S(1)} %add_convert_fusion.4), channel_id=1, source_target_pairs={{0,24},{1,25},{2,26},{3,27},{4,28},{5,29},{6,30},{7,31},{8,16},{9,... | collective-permute-start | bytes 55304 | tf_op jit(solution)/shard_map/ppermute | solution.py:40
  29.7 3.0 %collective-permute-done.10 = bf16[32,4096]{1,0:T(8,128)(2,1)S(1)} collective-permute-done((bf16[32,4096]{1,0:T(8,128)(2,1)S(1)}, bf16[32,4096]{1,0:T(8,128)(2,1)S(1)}, u32[]{:S(2)}, u32[]{:S(2)}) %collective-permute-start.10) | collective-permute-done | bytes 262176 | tf_op jit(solution)/shard_map/ppermute | solution.py:40
  40.6 2.4 %collective-permute-start.16 = (bf16[4,4,72,128]{3,2,1,0:T(8,128)(2,1)S(1)}, bf16[4,4,72,128]{3,2,1,0:T(8,128)(2,1)S(1)}, u32[]{:S(2)}, u32[]{:S(2)}) collective-permute-start(bf16[4,4,72,128]{3,2,1,0:T(8,128)(2,1)S(1)} %pad_maximum_fusion.2.refs_7_), channel_id=1, source_target_pairs={{0,1},{1,0},{2,3},{3,2},{4,5},{5,4},{6,7},{7,6},{8,9},{9,8},{10,11... | collective-permute-start | bytes 884744 | tf_op jit(solution)/shard_map/ppermute | solution.py:40
  44.3 4.6 %layer.4 = (bf16[72,256]{1,0:T(8,128)(2,1)S(1)}, bf16[72,512]{1,0:T(8,128)(2,1)S(1)}, bf16[4,72,512]{2,1,0:T(8,128)(2,1)S(1)}, bf16[72,256]{1,0:T(8,128)(2,1)S(1...) custom-call(f32[1,4]{1,0:T(1,128)S(1)} %copy-done.9, f32[1,4]{1,0:T(1,128)S(1)} %copy-done.10, ...), custom_call_target="tpu_custom_call" | custom-call | tf_op jit(solution)/shard_map/layer/pallas_call | solution.py:478
  58.2 3.3 %collective-permute-start.25 = (bf16[72,512]{1,0:T(8,128)(2,1)S(1)}, bf16[72,512]{1,0:T(8,128)(2,1)S(1)}, u32[]{:S(2)}, u32[]{:S(2)}) collective-permute-start(bf16[72,512]{1,0:T(8,128)(2,1)S(1)} %fusion.17), channel_id=1, source_target_pairs={{0,56},{1,57},{2,58},{3,59},{4,60},{5,61},{6,62},{7,63},{8,48},{9,... | collective-permute-start | bytes 221192 | tf_op jit(solution)/shard_map/ppermute | solution.py:40
  64.8 3.5 %collective-permute-done.24 = bf16[72,512]{1,0:T(8,128)(2,1)S(1)} collective-permute-done((bf16[72,512]{1,0:T(8,128)(2,1)S(1)}, bf16[72,512]{1,0:T(8,128)(2,1)S(1)}, u32[]{:S(2)}, u32[]{:S(2)}) %collective-permute-start.24) | collective-permute-done | bytes 73760 | tf_op jit(solution)/shard_map/ppermute | solution.py:40
  76.1 4.0 %collective-permute-start.29 = (bf16[4,72,512]{2,1,0:T(8,128)(2,1)S(1)}, bf16[4,72,512]{2,1,0:T(8,128)(2,1)S(1)}, u32[]{:S(2)}, u32[]{:S(2)}) collective-permute-start(bf16[4,72,512]{2,1,0:T(8,128)(2,1)S(1)} %pad_maximum_fusion.3.refs_7_), channel_id=1, source_target_pairs={{0,1},{1,0},{2,3},{3,2},{4,5},{5,4},{6,7},{7,6},{8,9},{9,8},{10,11... | collective-permute-start | bytes 884744 | tf_op jit(solution)/shard_map/ppermute | solution.py:40
  81.3 3.1 %layer.5 = (bf16[72,256]{1,0:T(8,128)(2,1)S(1)}, bf16[72,512]{1,0:T(8,128)(2,1)S(1)}, bf16[4,72,512]{2,1,0:T(8,128)(2,1)S(1)}, bf16[72,256]{1,0:T(8,128)(2,1)S(1...) custom-call(f32[1,4]{1,0:T(1,128)S(1)} %copy-done.9, f32[1,4]{1,0:T(1,128)S(1)} %copy-done.10, ...), custom_call_target="tpu_custom_call" | custom-call | tf_op jit(solution)/shard_map/layer/pallas_call | solution.py:478
  99.5 2.8 %collective-permute-done.36 = bf16[72,512]{1,0:T(8,128)(2,1)S(1)} collective-permute-done((bf16[72,512]{1,0:T(8,128)(2,1)S(1)}, bf16[72,512]{1,0:T(8,128)(2,1)S(1)}, u32[]{:S(2)}, u32[]{:S(2)}) %collective-permute-start.36) | collective-permute-done | bytes 73760 | tf_op jit(solution)/shard_map/ppermute | solution.py:40
  110.1 3.4 %collective-permute-start.41 = (bf16[4,72,512]{2,1,0:T(8,128)(2,1)S(1)}, bf16[4,72,512]{2,1,0:T(8,128)(2,1)S(1)}, u32[]{:S(2)}, u32[]{:S(2)}) collective-permute-start(bf16[4,72,512]{2,1,0:T(8,128)(2,1)S(1)} %pad_maximum_fusion.4.refs_7_), channel_id=1, source_target_pairs={{0,1},{1,0},{2,3},{3,2},{4,5},{5,4},{6,7},{7,6},{8,9},{9,8},{10,11... | collective-permute-start | bytes 884744 | tf_op jit(solution)/shard_map/ppermute | solution.py:40
  114.7 3.1 %layer.6 = (bf16[72,256]{1,0:T(8,128)(2,1)S(1)}, bf16[72,512]{1,0:T(8,128)(2,1)S(1)}, bf16[4,72,512]{2,1,0:T(8,128)(2,1)S(1)}, bf16[72,256]{1,0:T(8,128)(2,1)S(1...) custom-call(f32[1,4]{1,0:T(1,128)S(1)} %copy-done.9, f32[1,4]{1,0:T(1,128)S(1)} %copy-done.10, ...), custom_call_target="tpu_custom_call" | custom-call | tf_op jit(solution)/shard_map/layer/pallas_call | solution.py:478
  120.4 2.2 %collective-permute-start.44 = (bf16[72,512]{1,0:T(8,128)(2,1)S(1)}, bf16[72,512]{1,0:T(8,128)(2,1)S(1)}, u32[]{:S(2)}, u32[]{:S(2)}) collective-permute-start(bf16[72,512]{1,0:T(8,128)(2,1)S(1)} %get-tuple-element.125), channel_id=1, source_target_pairs={{0,4},{1,5},{2,6},{3,7},{4,0},{5,1},{6,2},{7,3},{8,12},{9,13},{10,... | collective-permute-start | bytes 221192 | tf_op jit(solution)/shard_map/ppermute | solution.py:40
  133.4 2.7 %collective-permute-done.48 = bf16[72,512]{1,0:T(8,128)(2,1)S(1)} collective-permute-done((bf16[72,512]{1,0:T(8,128)(2,1)S(1)}, bf16[72,512]{1,0:T(8,128)(2,1)S(1)}, u32[]{:S(2)}, u32[]{:S(2)}) %collective-permute-start.48) | collective-permute-done | bytes 73760 | tf_op jit(solution)/shard_map/ppermute | solution.py:40
  143.4 4.1 %collective-permute-start.53 = (bf16[4,72,512]{2,1,0:T(8,128)(2,1)S(1)}, bf16[4,72,512]{2,1,0:T(8,128)(2,1)S(1)}, u32[]{:S(2)}, u32[]{:S(2)}) collective-permute-start(bf16[4,72,512]{2,1,0:T(8,128)(2,1)S(1)} %pad_maximum_fusion.5.refs_7_), channel_id=1, source_target_pairs={{0,1},{1,0},{2,3},{3,2},{4,5},{5,4},{6,7},{7,6},{8,9},{9,8},{10,11... | collective-permute-start | bytes 884744 | tf_op jit(solution)/shard_map/ppermute | solution.py:40
  148.7 3.1 %layer.7 = (bf16[96,256]{1,0:T(8,128)(2,1)S(1)}, bf16[24,2048]{1,0:T(8,128)(2,1)S(1)}, bf16[4,24,2048]{2,1,0:T(8,128)(2,1)S(1)}, bf16[72,256]{1,0:T(8,128)(2,1)S...) custom-call(f32[1,4]{1,0:T(1,128)S(1)} %copy-done.9, f32[1,4]{1,0:T(1,128)S(1)} %copy-done.10, ...), custom_call_target="tpu_custom_call" | custom-call | tf_op jit(solution)/shard_map/layer/pallas_call | solution.py:478
  153.6 5.3 %collective-permute-done.55.refs_2_ = bf16[2,2048,128]{2,1,0:T(8,128)(2,1)S(1)} collective-permute-done((bf16[2,2048,128]{2,1,0:T(8,128)(2,1)S(1)}, bf16[2,2048,128]{2,1,0:T(8,128)(2,1)S(1)}, u32[]{:S(2)}, u32[]{:S(2)}) %collective-permute-start.55) | collective-permute-done | bytes 1048608 | tf_op jit(solution)/shard_map/ppermute | solution.py:40
  167.3 2.7 %collective-permute-start.60 = (bf16[24,2048]{1,0:T(8,128)(2,1)S(1)}, bf16[24,2048]{1,0:T(8,128)(2,1)S(1)}, u32[]{:S(2)}, u32[]{:S(2)}) collective-permute-start(bf16[24,2048]{1,0:T(8,128)(2,1)S(1)} %fusion.5), channel_id=1, source_target_pairs={{0,16},{1,17},{2,18},{3,19},{4,20},{5,21},{6,22},{7,23},{8,24},{9,... | collective-permute-start | bytes 294920 | tf_op jit(solution)/shard_map/ppermute | solution.py:40
  178.1 9.5 %collective-permute-done.63 = bf16[24,2048]{1,0:T(8,128)(2,1)S(1)} collective-permute-done((bf16[24,2048]{1,0:T(8,128)(2,1)S(1)}, bf16[24,2048]{1,0:T(8,128)(2,1)S(1)}, u32[]{:S(2)}, u32[]{:S(2)}) %collective-permute-start.63) | collective-permute-done | bytes 98336 | tf_op jit(solution)/shard_map/ppermute | solution.py:40
  187.6 6.9 %collective-permute-start.66 = (bf16[24,2048]{1,0:T(8,128)(2,1)S(1)}, bf16[24,2048]{1,0:T(8,128)(2,1)S(1)}, u32[]{:S(2)}, u32[]{:S(2)}) collective-permute-start(bf16[24,2048]{1,0:T(8,128)(2,1)S(1)} %add_add_fusion.own_ref), channel_id=1, source_target_pairs={{0,1},{1,0},{2,3},{3,2},{4,5},{5,4},{6,7},{7,6},{8,9},{9,8},{10,11... | collective-permute-start | bytes 294920 | tf_op jit(solution)/shard_map/ppermute | solution.py:40
  (196 shorter events, 110.1 us)
Async XLA Ops:
  0.7 14.8 %collective-permute-start.3 = (bf16[2048,128]{1,0:T(8,128)(2,1)}, bf16[2048,128]{1,0:T(8,128)(2,1)S(1)}, u32[]{:S(2)}, u32[]{:S(2)}) collective-permute-start(bf16[2048,128]{1,0:T(8,128)(2,1)} %refs_0_.11), channel_id=1, source_target_pairs={{0,96},{1,97},{2,98},{3,99},{4,100},{5,101},{6,102},{7,103},{8,104... | collective-permute-start | bytes 1572872 | tf_op jit(solution)/shard_map/ppermute | solution.py:40
  3.6 8.6 %collective-permute-start = (bf16[16,4096]{1,0:T(8,128)(2,1)S(1)}, bf16[16,4096]{1,0:T(8,128)(2,1)S(1)}, u32[]{:S(2)}, u32[]{:S(2)}) collective-permute-start(bf16[16,4096]{1,0:T(8,128)(2,1)S(1)} %get-tuple-element.118), channel_id=1, source_target_pairs={{0,8},{1,9},{2,10},{3,11},{4,12},{5,13},{6,14},{7,15},{8,0},{9,1},... | collective-permute-start | bytes 393224 | tf_op jit(solution)/shard_map/ppermute | solution.py:40
  5.0 7.7 %collective-permute-start.1 = (bf16[16,4096]{1,0:T(8,128)(2,1)S(1)}, bf16[16,4096]{1,0:T(8,128)(2,1)S(1)}, u32[]{:S(2)}, u32[]{:S(2)}) collective-permute-start(bf16[16,4096]{1,0:T(8,128)(2,1)S(1)} %get-tuple-element.117), channel_id=1, source_target_pairs={{0,16},{1,17},{2,18},{3,19},{4,20},{5,21},{6,22},{7,23},{8,24},{9,... | collective-permute-start | bytes 393224 | tf_op jit(solution)/shard_map/ppermute | solution.py:40
  7.6 7.9 %collective-permute-start.2 = (bf16[16,4096]{1,0:T(8,128)(2,1)S(1)}, bf16[16,4096]{1,0:T(8,128)(2,1)S(1)}, u32[]{:S(2)}, u32[]{:S(2)}) collective-permute-start(bf16[16,4096]{1,0:T(8,128)(2,1)S(1)} %get-tuple-element.116), channel_id=1, source_target_pairs={{0,24},{1,25},{2,26},{3,27},{4,28},{5,29},{6,30},{7,31},{8,16},{9,... | collective-permute-start | bytes 393224 | tf_op jit(solution)/shard_map/ppermute | solution.py:40
  15.5 6.1 %collective-permute-start.6 = (bf16[72,128]{1,0:T(8,128)(2,1)S(1)}, bf16[72,128]{1,0:T(8,128)(2,1)S(1)}, u32[]{:S(2)}, u32[]{:S(2)}) collective-permute-start(bf16[72,128]{1,0:T(8,128)(2,1)S(1)} %look.1), channel_id=1, source_target_pairs={{0,64},{1,65},{2,66},{3,67},{4,68},{5,69},{6,70},{7,71},{8,72},{9,... | collective-permute-start | bytes 55304 | tf_op jit(solution)/shard_map/ppermute | solution.py:40
  18.9 13.8 %collective-permute-start.11 = (bf16[32,4096]{1,0:T(8,128)(2,1)}, bf16[32,4096]{1,0:T(8,128)(2,1)S(1)}, u32[]{:S(2)}, u32[]{:S(2)}) collective-permute-start(bf16[32,4096]{1,0:T(8,128)(2,1)} %pad_maximum_fusion.7), channel_id=1, source_target_pairs={{0,4},{1,5},{2,6},{3,7},{4,0},{5,1},{6,2},{7,3},{8,12},{9,13},{10,... | collective-permute-start | bytes 786440 | tf_op jit(solution)/shard_map/ppermute | solution.py:40
  21.6 12.9 %collective-permute-start.12 = (bf16[32,4096]{1,0:T(8,128)(2,1)}, bf16[32,4096]{1,0:T(8,128)(2,1)S(1)}, u32[]{:S(2)}, u32[]{:S(2)}) collective-permute-start(bf16[32,4096]{1,0:T(8,128)(2,1)} %pad_maximum_fusion.7), channel_id=1, source_target_pairs={{0,6},{1,7},{2,4},{3,5},{4,2},{5,3},{6,0},{7,1},{8,14},{9,15},{10,... | collective-permute-start | bytes 786440 | tf_op jit(solution)/shard_map/ppermute | solution.py:40
  24.4 8.4 %collective-permute-start.10 = (bf16[32,4096]{1,0:T(8,128)(2,1)S(1)}, bf16[32,4096]{1,0:T(8,128)(2,1)S(1)}, u32[]{:S(2)}, u32[]{:S(2)}) collective-permute-start(bf16[32,4096]{1,0:T(8,128)(2,1)S(1)} %pad_maximum_fusion.6), channel_id=1, source_target_pairs={{0,2},{1,3},{2,0},{3,1},{4,6},{5,7},{6,4},{7,5},{8,10},{9,11},{10,... | collective-permute-start | bytes 786440 | tf_op jit(solution)/shard_map/ppermute | solution.py:40
  58.2 6.6 %collective-permute-start.25 = (bf16[72,512]{1,0:T(8,128)(2,1)S(1)}, bf16[72,512]{1,0:T(8,128)(2,1)S(1)}, u32[]{:S(2)}, u32[]{:S(2)}) collective-permute-start(bf16[72,512]{1,0:T(8,128)(2,1)S(1)} %fusion.17), channel_id=1, source_target_pairs={{0,56},{1,57},{2,58},{3,59},{4,60},{5,61},{6,62},{7,63},{8,48},{9,... | collective-permute-start | bytes 221192 | tf_op jit(solution)/shard_map/ppermute | solution.py:40
  61.5 6.8 %collective-permute-start.24 = (bf16[72,512]{1,0:T(8,128)(2,1)S(1)}, bf16[72,512]{1,0:T(8,128)(2,1)S(1)}, u32[]{:S(2)}, u32[]{:S(2)}) collective-permute-start(bf16[72,512]{1,0:T(8,128)(2,1)S(1)} %fusion.17), channel_id=1, source_target_pairs={{0,48},{1,49},{2,50},{3,51},{4,52},{5,53},{6,54},{7,55},{8,56},{9,... | collective-permute-start | bytes 221192 | tf_op jit(solution)/shard_map/ppermute | solution.py:40
  62.6 5.7 %collective-permute-start.23 = (bf16[72,512]{1,0:T(8,128)(2,1)S(1)}, bf16[72,512]{1,0:T(8,128)(2,1)S(1)}, u32[]{:S(2)}, u32[]{:S(2)}) collective-permute-start(bf16[72,512]{1,0:T(8,128)(2,1)S(1)} %fusion.17), channel_id=1, source_target_pairs={{0,40},{1,41},{2,42},{3,43},{4,44},{5,45},{6,46},{7,47},{8,32},{9,... | collective-permute-start | bytes 221192 | tf_op jit(solution)/shard_map/ppermute | solution.py:40
  63.5 6.2 %collective-permute-start.22 = (bf16[72,512]{1,0:T(8,128)(2,1)S(1)}, bf16[72,512]{1,0:T(8,128)(2,1)S(1)}, u32[]{:S(2)}, u32[]{:S(2)}) collective-permute-start(bf16[72,512]{1,0:T(8,128)(2,1)S(1)} %fusion.17), channel_id=1, source_target_pairs={{0,32},{1,33},{2,34},{3,35},{4,36},{5,37},{6,38},{7,39},{8,40},{9,... | collective-permute-start | bytes 221192 | tf_op jit(solution)/shard_map/ppermute | solution.py:40
  92.9 6.6 %collective-permute-start.37 = (bf16[72,512]{1,0:T(8,128)(2,1)S(1)}, bf16[72,512]{1,0:T(8,128)(2,1)S(1)}, u32[]{:S(2)}, u32[]{:S(2)}) collective-permute-start(bf16[72,512]{1,0:T(8,128)(2,1)S(1)} %fusion.13), channel_id=1, source_target_pairs={{0,56},{1,57},{2,58},{3,59},{4,60},{5,61},{6,62},{7,63},{8,48},{9,... | collective-permute-start | bytes 221192 | tf_op jit(solution)/shard_map/ppermute | solution.py:40
  94.9 7.5 %collective-permute-start.36 = (bf16[72,512]{1,0:T(8,128)(2,1)S(1)}, bf16[72,512]{1,0:T(8,128)(2,1)S(1)}, u32[]{:S(2)}, u32[]{:S(2)}) collective-permute-start(bf16[72,512]{1,0:T(8,128)(2,1)S(1)} %fusion.13), channel_id=1, source_target_pairs={{0,48},{1,49},{2,50},{3,51},{4,52},{5,53},{6,54},{7,55},{8,56},{9,... | collective-permute-start | bytes 221192 | tf_op jit(solution)/shard_map/ppermute | solution.py:40
  95.8 6.5 %collective-permute-start.35 = (bf16[72,512]{1,0:T(8,128)(2,1)S(1)}, bf16[72,512]{1,0:T(8,128)(2,1)S(1)}, u32[]{:S(2)}, u32[]{:S(2)}) collective-permute-start(bf16[72,512]{1,0:T(8,128)(2,1)S(1)} %fusion.13), channel_id=1, source_target_pairs={{0,40},{1,41},{2,42},{3,43},{4,44},{5,45},{6,46},{7,47},{8,32},{9,... | collective-permute-start | bytes 221192 | tf_op jit(solution)/shard_map/ppermute | solution.py:40
  97.4 6.4 %collective-permute-start.34 = (bf16[72,512]{1,0:T(8,128)(2,1)S(1)}, bf16[72,512]{1,0:T(8,128)(2,1)S(1)}, u32[]{:S(2)}, u32[]{:S(2)}) collective-permute-start(bf16[72,512]{1,0:T(8,128)(2,1)S(1)} %fusion.13), channel_id=1, source_target_pairs={{0,32},{1,33},{2,34},{3,35},{4,36},{5,37},{6,38},{7,39},{8,40},{9,... | collective-permute-start | bytes 221192 | tf_op jit(solution)/shard_map/ppermute | solution.py:40
  126.8 6.6 %collective-permute-start.49 = (bf16[72,512]{1,0:T(8,128)(2,1)S(1)}, bf16[72,512]{1,0:T(8,128)(2,1)S(1)}, u32[]{:S(2)}, u32[]{:S(2)}) collective-permute-start(bf16[72,512]{1,0:T(8,128)(2,1)S(1)} %fusion.9), channel_id=1, source_target_pairs={{0,56},{1,57},{2,58},{3,59},{4,60},{5,61},{6,62},{7,63},{8,48},{9,... | collective-permute-start | bytes 221192 | tf_op jit(solution)/shard_map/ppermute | solution.py:40
  128.9 7.2 %collective-permute-start.48 = (bf16[72,512]{1,0:T(8,128)(2,1)S(1)}, bf16[72,512]{1,0:T(8,128)(2,1)S(1)}, u32[]{:S(2)}, u32[]{:S(2)}) collective-permute-start(bf16[72,512]{1,0:T(8,128)(2,1)S(1)} %fusion.9), channel_id=1, source_target_pairs={{0,48},{1,49},{2,50},{3,51},{4,52},{5,53},{6,54},{7,55},{8,56},{9,... | collective-permute-start | bytes 221192 | tf_op jit(solution)/shard_map/ppermute | solution.py:40
  129.5 6.6 %collective-permute-start.47 = (bf16[72,512]{1,0:T(8,128)(2,1)S(1)}, bf16[72,512]{1,0:T(8,128)(2,1)S(1)}, u32[]{:S(2)}, u32[]{:S(2)}) collective-permute-start(bf16[72,512]{1,0:T(8,128)(2,1)S(1)} %fusion.9), channel_id=1, source_target_pairs={{0,40},{1,41},{2,42},{3,43},{4,44},{5,45},{6,46},{7,47},{8,32},{9,... | collective-permute-start | bytes 221192 | tf_op jit(solution)/shard_map/ppermute | solution.py:40
  136.5 22.4 %collective-permute-start.55 = (bf16[2,2048,128]{2,1,0:T(8,128)(2,1)S(1)}, bf16[2,2048,128]{2,1,0:T(8,128)(2,1)S(1)}, u32[]{:S(2)}, u32[]{:S(2)}) collective-permute-start(bf16[2,2048,128]{2,1,0:T(8,128)(2,1)S(1)} %pad_maximum_fusion.1), channel_id=1, source_target_pairs={{0,32},{1,33},{2,34},{3,35},{4,36},{5,37},{6,38},{7,39},{8,40},{9,... | collective-permute-start | bytes 3145736 | tf_op jit(solution)/shard_map/ppermute | solution.py:40
  165.7 6.0 %collective-permute-start.59 = (bf16[24,2048]{1,0:T(8,128)(2,1)S(1)}, bf16[24,2048]{1,0:T(8,128)(2,1)S(1)}, u32[]{:S(2)}, u32[]{:S(2)}) collective-permute-start(bf16[24,2048]{1,0:T(8,128)(2,1)S(1)} %fusion.5), channel_id=1, source_target_pairs={{0,8},{1,9},{2,10},{3,11},{4,12},{5,13},{6,14},{7,15},{8,0},{9,1},... | collective-permute-start | bytes 294920 | tf_op jit(solution)/shard_map/ppermute | solution.py:40
  167.3 5.8 %collective-permute-start.60 = (bf16[24,2048]{1,0:T(8,128)(2,1)S(1)}, bf16[24,2048]{1,0:T(8,128)(2,1)S(1)}, u32[]{:S(2)}, u32[]{:S(2)}) collective-permute-start(bf16[24,2048]{1,0:T(8,128)(2,1)S(1)} %fusion.5), channel_id=1, source_target_pairs={{0,16},{1,17},{2,18},{3,19},{4,20},{5,21},{6,22},{7,23},{8,24},{9,... | collective-permute-start | bytes 294920 | tf_op jit(solution)/shard_map/ppermute | solution.py:40
  176.8 10.8 %collective-permute-start.63 = (bf16[24,2048]{1,0:T(8,128)(2,1)S(1)}, bf16[24,2048]{1,0:T(8,128)(2,1)S(1)}, u32[]{:S(2)}, u32[]{:S(2)}) collective-permute-start(bf16[24,2048]{1,0:T(8,128)(2,1)S(1)} %add_convert_fusion), channel_id=1, source_target_pairs={{96,2},{97,3},{98,32},{99,33},{100,70},{101,71},{102,100},{103,101... | collective-permute-start | bytes 294920 | tf_op jit(solution)/shard_map/ppermute | solution.py:40
  187.6 7.9 %collective-permute-start.66 = (bf16[24,2048]{1,0:T(8,128)(2,1)S(1)}, bf16[24,2048]{1,0:T(8,128)(2,1)S(1)}, u32[]{:S(2)}, u32[]{:S(2)}) collective-permute-start(bf16[24,2048]{1,0:T(8,128)(2,1)S(1)} %add_add_fusion.own_ref), channel_id=1, source_target_pairs={{0,1},{1,0},{2,3},{3,2},{4,5},{5,4},{6,7},{7,6},{8,9},{9,8},{10,11... | collective-permute-start | bytes 294920 | tf_op jit(solution)/shard_map/ppermute | solution.py:40
  (58 other events, 303.1 us)
